TPU v7x, 256 devices: a whole 4x4x8 slice. The times are simulated.
256 devices in a mesh: seq: 16 (over z, core), fsdp: 16 (over x, y).
Axes of the slice: x: 4, y: 4, z: 8, core: 2. Of those that a mesh axis runs over, the one named last changes fastest.
Arguments:
- tokens: bfloat16 [2048, 8192], P('seq', 'fsdp'), may hold values from -6 to 6
- norm_gain: float32 [8192], replicated, may hold values from 0.25 to 1.75
- gate_proj: bfloat16 [8192, 8192], P('seq', 'fsdp'), may hold values from -0.0625 to 0.0625
- value_proj: bfloat16 [8192, 8192], P('seq', 'fsdp'), may hold values from -0.0625 to 0.0625
- step_proj: bfloat16 [8192, 128], P('seq', 'fsdp'), may hold values from -0.0625 to 0.0625
- state_proj: bfloat16 [8192, 4, 256], P('seq'), may hold values from -0.0625 to 0.0625
- conv_value: float32 [4, 8192], P(None, 'fsdp'), may hold values from -3 to 3
- conv_state: float32 [4, 4, 256], replicated, may hold values from -3 to 3
- step_bias: float32 [128], P('fsdp'), may hold values from -1 to 1
- decay_rate: float32 [128], P('fsdp'), may hold values from 0.00024414062 to 0.1
- skip_gain: float32 [128], P('fsdp'), may hold values from 0.5 to 1.5
- mix_gain: float32 [8192], P('fsdp'), may hold values from 0.25 to 1.75
- out_proj: bfloat16 [8192, 8192], P('fsdp', 'seq'), may hold values from -0.09375 to 0.09375
- doc_lengths: int32 [32], replicated, may hold values from 1 to 1024, 2048 in all
Outputs:
- layer_out: bfloat16 [2048, 8192], P('seq', 'fsdp')
Inputs may be any that keep to these rules, and one draw needn't show every extreme that they name: `doc_lengths`: the longest document has exactly 1024 tokens, so it spans many stretches; the lengths sum to 2048.
All inputs are finite; a program needn't handle non-finite values.
Results may differ from a plain program's by a relative error of at most 0.014.
Values may be sent and summed in bfloat16 or wider, within the bound.
A program may use at most 128 MiB of HBM per device.

v0:
```python
import jax
import jax.numpy as jnp
from jax import lax
from jax.sharding import PartitionSpec as P

H = 128
HEAD_DIM = 64
N = 128
G = 4


EPSILON = 1e-05
PRECISE = lax.Precision.HIGHEST


def from_behind(value, axis, steps):
    count = lax.axis_size(axis)
    leading, last = (max(0, -steps), min(count, count - steps))
    return lax.ppermute(value, axis, [(source, source + steps) for source in range(leading, last)])


def partner(block, axis, distance):
    count = lax.axis_size(axis)
    route = []
    for low in range(count):
        high = low | 1 << distance
        if high != low and high < count:
            route += [(low, high), (high, low)]
    return lax.ppermute(block, axis, route)


def local(
    tokens,
    norm_gain,
    gate_proj,
    value_proj,
    step_proj,
    state_proj,
    conv_value,
    conv_state,
    step_bias,
    decay_rate,
    skip_gain,
    mix_gain,
    out_proj,
    doc_lengths,
):
    span_rows = tokens.shape[0]
    seq_index = lax.axis_index("seq")
    fsdp_index = lax.axis_index("fsdp")
    head_count = step_bias.shape[0]
    inner_width = gate_proj.shape[1]
    group_devices = lax.axis_size("fsdp") // G
    group_index = fsdp_index // group_devices
    gathered = lax.all_gather(tokens, "fsdp", axis=1, tiled=True)
    as_float = gathered.astype(jnp.float32)
    normed = (
        as_float
        * lax.rsqrt(jnp.mean(as_float * as_float, axis=1, keepdims=True) + EPSILON)
        * norm_gain
    ).astype(jnp.bfloat16)
    state_cols = lax.dynamic_index_in_dim(state_proj, group_index, 1, keepdims=False)
    stacked = jnp.concatenate([gate_proj, value_proj, state_cols, step_proj], axis=1)
    spread = lax.all_to_all(normed, "seq", split_axis=1, concat_axis=0, tiled=True)
    summed = lax.psum_scatter(
        jnp.dot(spread, stacked, preferred_element_type=jnp.float32),
        "seq",
        scatter_dimension=0,
        tiled=True,
    )
    gate = summed[:, :inner_width]
    values = summed[:, inner_width : 2 * inner_width]
    states = summed[:, 2 * inner_width : 2 * inner_width + 2 * N]
    raw_step = summed[:, 2 * inner_width + 2 * N :]
    raw_mix = jnp.concatenate([values, states], axis=1).astype(jnp.bfloat16)
    tail_rows = from_behind(raw_mix[span_rows - 3 :], "seq", 1)
    extended = jnp.concatenate([tail_rows, raw_mix], axis=0)
    starts = jnp.cumsum(doc_lengths) - doc_lengths
    span_start = seq_index * span_rows
    positions = span_start - 3 + jnp.arange(span_rows + 3, dtype=jnp.int32)
    segment_ext = jnp.sum(starts[None, :] <= positions[:, None], axis=1) - 1
    segment = segment_ext[3:]
    taps = jnp.concatenate(
        [conv_value, lax.dynamic_index_in_dim(conv_state, group_index, 1, keepdims=False)], axis=1
    )
    convolved = jnp.zeros((span_rows, taps.shape[1]), jnp.float32)
    for offset in range(4):
        same_doc = segment_ext[offset : offset + span_rows] == segment
        convolved = (
            convolved
            + jnp.where(
                same_doc[:, None], extended[offset : offset + span_rows].astype(jnp.float32), 0.0
            )
            * taps[offset]
        )
    rounded = lax.optimization_barrier(jax.nn.silu(convolved).astype(jnp.bfloat16))
    activated = rounded.astype(jnp.float32)
    inputs = activated[:, :inner_width].reshape(span_rows, head_count, HEAD_DIM)
    in_map = activated[:, inner_width : inner_width + N]
    out_map = activated[:, inner_width + N :]
    in_half = rounded[:, inner_width : inner_width + N]
    out_half = rounded[:, inner_width + N :]
    step_size = jax.nn.softplus(raw_step + step_bias)
    log_decay = -decay_rate * step_size
    cumulative = jnp.cumsum(log_decay, axis=0)
    order = jnp.arange(span_rows)
    causal = (segment[:, None] == segment[None, :]) & (order[:, None] >= order[None, :])
    gaps = cumulative.T[:, :, None] - cumulative.T[:, None, :]
    decay = jnp.exp(jnp.where(causal[None], gaps, -jnp.inf))
    scores = jnp.dot(out_half, in_half.T, preferred_element_type=jnp.float32)
    mixing = decay * scores[None] * step_size.T[:, None, :]
    intra = jnp.einsum("hts,shp->thp", mixing, inputs, precision=PRECISE)
    last_segment = segment[span_rows - 1]
    prior_segment = segment_ext[2]
    in_last = segment == last_segment
    to_end = (
        jnp.where(in_last[:, None], jnp.exp(cumulative[span_rows - 1][None, :] - cumulative), 0.0)
        * step_size
    )
    local_state = jnp.einsum("sh,shp,sn->hpn", to_end, inputs, in_map, precision=PRECISE)
    passing = jnp.where(last_segment == prior_segment, jnp.exp(cumulative[span_rows - 1]), 0.0)
    empty = jnp.zeros_like(local_state)

    def relay(turn, incoming):
        return from_behind(
            (passing[:, None, None] * incoming + local_state).astype(jnp.bfloat16), "seq", 1
        ).astype(jnp.float32)

    incoming = lax.fori_loop(0, lax.axis_size("seq") - 1, relay, empty)
    carried = jnp.where((segment == prior_segment)[:, None], jnp.exp(cumulative), 0.0)
    from_state = (
        jnp.einsum("tn,hpn->thp", out_map, incoming, precision=PRECISE) * carried[:, :, None]
    )
    outputs = intra + from_state + skip_gain[None, :, None] * inputs
    gated = outputs.reshape(span_rows, inner_width) * jax.nn.silu(gate)
    squares = jnp.sum(gated * gated, axis=1)
    for bit in range(group_devices.bit_length() - 1):
        squares = squares + partner(squares, "fsdp", bit)
    scaled = (
        gated * lax.rsqrt(squares[:, None] / (H * HEAD_DIM // G) + EPSILON) * mix_gain
    ).astype(jnp.bfloat16)
    terms = jnp.dot(
        scaled,
        lax.all_gather(out_proj, "seq", axis=1, tiled=True),
        preferred_element_type=jnp.float32,
    )
    mixed = lax.psum_scatter(
        terms.astype(jnp.bfloat16), "fsdp", scatter_dimension=1, tiled=True
    ).astype(jnp.float32)
    return (tokens.astype(jnp.float32) + mixed).astype(jnp.bfloat16)


def solution(mesh):
    return jax.shard_map(
        local,
        mesh=mesh,
        in_specs=(
            P("seq", "fsdp"),
            P(),
            P("seq", "fsdp"),
            P("seq", "fsdp"),
            P("seq", "fsdp"),
            P("seq", None, None),
            P(None, "fsdp"),
            P(),
            P("fsdp"),
            P("fsdp"),
            P("fsdp"),
            P("fsdp"),
            P("fsdp", "seq"),
            P(),
        ),
        out_specs=P("seq", "fsdp"),
        check_vma=False,
    )
```

profile of v0, /device:TPU:4, one launch (start us, length us, event | category | flops | bytes accessed | tf_op | source)
XLA Modules:
  0.0 451.4 jit_solution(12349447251498023610)
XLA Ops:
  8.3 53.5 %all-gather.3.cloned.1.call-done = bf16[128,8192]{0,1:T(8,128)(2,1)} async-done(((bf16[128,512]{0,1:T(8,128)(2,1)}), bf16[128,8192]{0,1:T(8,128)(2,1)}) %all-gather.3.cloned.1.call-update) | async-done | bytes 2097168 | tf_op jit(solution)/shard_map/all_gather | solution.py:55
  64.7 4.6 %fusion.4 = bf16[128,8192]{0,1:T(8,128)(2,1)} fusion(bf16[128,8192]{0,1:T(8,128)(2,1)S(1)} %copy-done.1, f32[8192]{0:T(1024)} %param.17, f32[128]{0:T(128)S(1)} %add_rsqrt_fusion.1), kind=kLoop, calls=%fused_computation.8 | loop fusion | flops 4194304 | bytes 4227584 | tf_op jit(solution)/shard_map/convert_element_type | solution.py:61
  69.2 7.2 %all-to-all-start = ((bf16[128,16,512]{0,2,1:T(8,128)(2,1)}), bf16[128,16,512]{0,2,1:T(8,128)(2,1)S(1)}, u32[]{:S(2)}, u32[]{:S(2)}) async-start(bf16[128,16,512]{0,2,1:T(8,128)(2,1)} %bitcast.36), calls=%async_computation | async-start | bytes 4194304 | tf_op jit(solution)/shard_map/all_to_all | solution.py:64
  77.3 48.3 %all-to-all-done = bf16[128,16,512]{0,2,1:T(8,128)(2,1)S(1)} async-done(((bf16[128,16,512]{0,2,1:T(8,128)(2,1)}), bf16[128,16,512]{0,2,1:T(8,128)(2,1)S(1)}, u32[]{:S(2)}, u32[]{:S(2)}) %all-to-all-start) | async-done | bytes 2097184 | tf_op jit(solution)/shard_map/all_to_all | solution.py:64
  128.3 8.8 %fusion.5 = f32[2048,1288]{0,1:T(8,128)} fusion(bf16[2048,512]{1,0:T(8,128)(2,1)} %bitcast.37, bf16[512,8]{1,0:T(8,128)(2,1)S(1)} %copy.48, bf16[512,256]{1,0:T(8,128)(2,1)S(1)} %bitcast.42, bf16[512,512]{1,0:T(8,128)(2,1)} %param.19, bf16[512,512]{1,0:T(8,128)(2,1)} %param.18), kind=kOutput, calls=%fused_computation.9 | convolution fusion | flops 2706407424 | bytes 13967360 | tf_op jit(solution)/shard_map/dot_general | solution.py:66
  142.4 67.5 %reduce-scatter.3.cloned.1.call-done = f32[128,1288]{0,1:T(8,128)} async-done(((f32[2048,1288]{0,1:T(8,128)}), f32[128,1288]{0,1:T(8,128)}) %reduce-scatter.3.cloned.1.call-update) | async-done | bytes 659472 | tf_op jit(solution)/shard_map/reduce_scatter | solution.py:65
  216.7 107.3 %while.11 = (s32[]{:T(128)}, f32[8,64,128]{2,1,0:T(8,128)S(1)}, f32[8]{0:T(128)S(1)}, f32[8,64,128]{2,1,0:T(8,128)S(1)}, s32[]{:T(128)}, /*index=5*/s32[]{:T(128)}) while((s32[]{:T(128)}, f32[8,64,128]{2,1,0:T(8,128)S(1)}, f32[8]{0:T(128)S(1)}, f32[8,64,128]{2,1,0:T(8,128)S(1)}, s32[]{:T(128)}, /*index=5*/s32[]{:T(128)}) %tuple.33), condition=%wide.region_6.7_spmd.clone, body=%wide.region_5.6_spmd.clone.sunk | while | flops 327683 | bytes 1573015 | solution.py:129
  220.2 5.8 %collective-permute-start = (bf16[8,64,128]{2,1,0:T(8,128)(2,1)S(1)}, bf16[8,64,128]{2,1,0:T(8,128)(2,1)S(1)}, u32[]{:S(2)}, u32[]{:S(2)}) collective-permute-start(bf16[8,64,128]{2,1,0:T(8,128)(2,1)S(1)} %fusion.56), channel_id=1, source_target_pairs={{0,16},{16,32},{32,48},{48,64},{64,80},{80,96},{96,112},{112,128},... | collective-permute-start | bytes 393224 | tf_op jit(solution)/shard_map/while/body/eval_jaxpr/ppermute | solution.py:19
  227.1 7.9 %collective-permute-start = (bf16[8,64,128]{2,1,0:T(8,128)(2,1)S(1)}, bf16[8,64,128]{2,1,0:T(8,128)(2,1)S(1)}, u32[]{:S(2)}, u32[]{:S(2)}) collective-permute-start(bf16[8,64,128]{2,1,0:T(8,128)(2,1)S(1)} %fusion.56), channel_id=1, source_target_pairs={{0,16},{16,32},{32,48},{48,64},{64,80},{80,96},{96,112},{112,128},... | collective-permute-start | bytes 393224 | tf_op jit(solution)/shard_map/while/body/eval_jaxpr/ppermute | solution.py:19
  236.1 8.1 %collective-permute-start = (bf16[8,64,128]{2,1,0:T(8,128)(2,1)S(1)}, bf16[8,64,128]{2,1,0:T(8,128)(2,1)S(1)}, u32[]{:S(2)}, u32[]{:S(2)}) collective-permute-start(bf16[8,64,128]{2,1,0:T(8,128)(2,1)S(1)} %fusion.56), channel_id=1, source_target_pairs={{0,16},{16,32},{32,48},{48,64},{64,80},{80,96},{96,112},{112,128},... | collective-permute-start | bytes 393224 | tf_op jit(solution)/shard_map/while/body/eval_jaxpr/ppermute | solution.py:19
  245.3 8.1 %collective-permute-start = (bf16[8,64,128]{2,1,0:T(8,128)(2,1)S(1)}, bf16[8,64,128]{2,1,0:T(8,128)(2,1)S(1)}, u32[]{:S(2)}, u32[]{:S(2)}) collective-permute-start(bf16[8,64,128]{2,1,0:T(8,128)(2,1)S(1)} %fusion.56), channel_id=1, source_target_pairs={{0,16},{16,32},{32,48},{48,64},{64,80},{80,96},{96,112},{112,128},... | collective-permute-start | bytes 393224 | tf_op jit(solution)/shard_map/while/body/eval_jaxpr/ppermute | solution.py:19
  254.5 8.1 %collective-permute-start = (bf16[8,64,128]{2,1,0:T(8,128)(2,1)S(1)}, bf16[8,64,128]{2,1,0:T(8,128)(2,1)S(1)}, u32[]{:S(2)}, u32[]{:S(2)}) collective-permute-start(bf16[8,64,128]{2,1,0:T(8,128)(2,1)S(1)} %fusion.56), channel_id=1, source_target_pairs={{0,16},{16,32},{32,48},{48,64},{64,80},{80,96},{96,112},{112,128},... | collective-permute-start | bytes 393224 | tf_op jit(solution)/shard_map/while/body/eval_jaxpr/ppermute | solution.py:19
  263.8 7.7 %collective-permute-start = (bf16[8,64,128]{2,1,0:T(8,128)(2,1)S(1)}, bf16[8,64,128]{2,1,0:T(8,128)(2,1)S(1)}, u32[]{:S(2)}, u32[]{:S(2)}) collective-permute-start(bf16[8,64,128]{2,1,0:T(8,128)(2,1)S(1)} %fusion.56), channel_id=1, source_target_pairs={{0,16},{16,32},{32,48},{48,64},{64,80},{80,96},{96,112},{112,128},... | collective-permute-start | bytes 393224 | tf_op jit(solution)/shard_map/while/body/eval_jaxpr/ppermute | solution.py:19
  272.6 5.4 %collective-permute-start = (bf16[8,64,128]{2,1,0:T(8,128)(2,1)S(1)}, bf16[8,64,128]{2,1,0:T(8,128)(2,1)S(1)}, u32[]{:S(2)}, u32[]{:S(2)}) collective-permute-start(bf16[8,64,128]{2,1,0:T(8,128)(2,1)S(1)} %fusion.56), channel_id=1, source_target_pairs={{0,16},{16,32},{32,48},{48,64},{64,80},{80,96},{96,112},{112,128},... | collective-permute-start | bytes 393224 | tf_op jit(solution)/shard_map/while/body/eval_jaxpr/ppermute | solution.py:19
  279.0 5.3 %collective-permute-start = (bf16[8,64,128]{2,1,0:T(8,128)(2,1)S(1)}, bf16[8,64,128]{2,1,0:T(8,128)(2,1)S(1)}, u32[]{:S(2)}, u32[]{:S(2)}) collective-permute-start(bf16[8,64,128]{2,1,0:T(8,128)(2,1)S(1)} %fusion.56), channel_id=1, source_target_pairs={{0,16},{16,32},{32,48},{48,64},{64,80},{80,96},{96,112},{112,128},... | collective-permute-start | bytes 393224 | tf_op jit(solution)/shard_map/while/body/eval_jaxpr/ppermute | solution.py:19
  285.5 5.3 %collective-permute-start = (bf16[8,64,128]{2,1,0:T(8,128)(2,1)S(1)}, bf16[8,64,128]{2,1,0:T(8,128)(2,1)S(1)}, u32[]{:S(2)}, u32[]{:S(2)}) collective-permute-start(bf16[8,64,128]{2,1,0:T(8,128)(2,1)S(1)} %fusion.56), channel_id=1, source_target_pairs={{0,16},{16,32},{32,48},{48,64},{64,80},{80,96},{96,112},{112,128},... | collective-permute-start | bytes 393224 | tf_op jit(solution)/shard_map/while/body/eval_jaxpr/ppermute | solution.py:19
  291.9 5.3 %collective-permute-start = (bf16[8,64,128]{2,1,0:T(8,128)(2,1)S(1)}, bf16[8,64,128]{2,1,0:T(8,128)(2,1)S(1)}, u32[]{:S(2)}, u32[]{:S(2)}) collective-permute-start(bf16[8,64,128]{2,1,0:T(8,128)(2,1)S(1)} %fusion.56), channel_id=1, source_target_pairs={{0,16},{16,32},{32,48},{48,64},{64,80},{80,96},{96,112},{112,128},... | collective-permute-start | bytes 393224 | tf_op jit(solution)/shard_map/while/body/eval_jaxpr/ppermute | solution.py:19
  298.3 5.3 %collective-permute-start = (bf16[8,64,128]{2,1,0:T(8,128)(2,1)S(1)}, bf16[8,64,128]{2,1,0:T(8,128)(2,1)S(1)}, u32[]{:S(2)}, u32[]{:S(2)}) collective-permute-start(bf16[8,64,128]{2,1,0:T(8,128)(2,1)S(1)} %fusion.56), channel_id=1, source_target_pairs={{0,16},{16,32},{32,48},{48,64},{64,80},{80,96},{96,112},{112,128},... | collective-permute-start | bytes 393224 | tf_op jit(solution)/shard_map/while/body/eval_jaxpr/ppermute | solution.py:19
  304.7 5.3 %collective-permute-start = (bf16[8,64,128]{2,1,0:T(8,128)(2,1)S(1)}, bf16[8,64,128]{2,1,0:T(8,128)(2,1)S(1)}, u32[]{:S(2)}, u32[]{:S(2)}) collective-permute-start(bf16[8,64,128]{2,1,0:T(8,128)(2,1)S(1)} %fusion.56), channel_id=1, source_target_pairs={{0,16},{16,32},{32,48},{48,64},{64,80},{80,96},{96,112},{112,128},... | collective-permute-start | bytes 393224 | tf_op jit(solution)/shard_map/while/body/eval_jaxpr/ppermute | solution.py:19
  311.2 5.3 %collective-permute-start = (bf16[8,64,128]{2,1,0:T(8,128)(2,1)S(1)}, bf16[8,64,128]{2,1,0:T(8,128)(2,1)S(1)}, u32[]{:S(2)}, u32[]{:S(2)}) collective-permute-start(bf16[8,64,128]{2,1,0:T(8,128)(2,1)S(1)} %fusion.56), channel_id=1, source_target_pairs={{0,16},{16,32},{32,48},{48,64},{64,80},{80,96},{96,112},{112,128},... | collective-permute-start | bytes 393224 | tf_op jit(solution)/shard_map/while/body/eval_jaxpr/ppermute | solution.py:19
  317.6 5.3 %collective-permute-start = (bf16[8,64,128]{2,1,0:T(8,128)(2,1)S(1)}, bf16[8,64,128]{2,1,0:T(8,128)(2,1)S(1)}, u32[]{:S(2)}, u32[]{:S(2)}) collective-permute-start(bf16[8,64,128]{2,1,0:T(8,128)(2,1)S(1)} %fusion.56), channel_id=1, source_target_pairs={{0,16},{16,32},{32,48},{48,64},{64,80},{80,96},{96,112},{112,128},... | collective-permute-start | bytes 393224 | tf_op jit(solution)/shard_map/while/body/eval_jaxpr/ppermute | solution.py:19
  328.9 3.0 collective-permute-start.3
  334.0 6.2 %convolution_convert_fusion = bf16[128,8192]{1,0:T(8,128)(2,1)} fusion(bf16[512,8192]{1,0:T(8,128)(2,1)} %all-gather.5.cloned.1.call-done, f32[128,512]{0,1:T(8,128)S(1)} %get-tuple-element.56, f32[512]{0:T(512)S(1)} %copy-done.3, f32[128]{0:T(128)S(1)} %add_rsqrt_fusion), kind=kOutput, calls=%fused_computation.3 | convolution fusion | flops 1074987008 | bytes 10750464 | tf_op jit(solution)/shard_map/dot_general | solution.py:142
  340.1 103.1 %reduce-scatter.5.cloned.1.call-done = bf16[128,512]{1,0:T(8,128)(2,1)} async-done(((bf16[128,8192]{1,0:T(8,128)(2,1)}), bf16[128,512]{1,0:T(8,128)(2,1)}) %reduce-scatter.5.cloned.1.call-update) | async-done | bytes 131088 | tf_op jit(solution)/shard_map/reduce_scatter | solution.py:147
  (124 shorter events, 45.7 us)
Async XLA Ops:
  6.5 55.3 %all-gather.3.cloned.1.call-start = ((), (), s32[]{:S(2)}) async-start(), calls=%async_computation.3 | async-start | bytes 2228224 | tf_op jit(solution)/shard_map/all_gather | solution.py:55
  69.2 56.4 %all-to-all-start = ((bf16[128,16,512]{0,2,1:T(8,128)(2,1)}), bf16[128,16,512]{0,2,1:T(8,128)(2,1)S(1)}, u32[]{:S(2)}, u32[]{:S(2)}) async-start(bf16[128,16,512]{0,2,1:T(8,128)(2,1)} %bitcast.36), calls=%async_computation | async-start | bytes 4194304 | tf_op jit(solution)/shard_map/all_to_all | solution.py:64
  76.5 133.5 %reduce-scatter.3.cloned.1.call-start = ((), (), s32[]{:S(2)}) async-start(), calls=%async_computation.4 | async-start | bytes 11210752 | tf_op jit(solution)/shard_map/reduce_scatter | solution.py:65
  137.1 196.9 %all-gather.5.cloned.1.call-start = ((), (), s32[]{:S(2)}) async-start(), calls=%async_computation.5 | async-start | bytes 8912896 | tf_op jit(solution)/shard_map/all_gather | solution.py:144
  137.8 305.4 %reduce-scatter.5.cloned.1.call-start = ((), (), s32[]{:S(2)}) async-start(), calls=%async_computation.6 | async-start | bytes 2228224 | tf_op jit(solution)/shard_map/reduce_scatter | solution.py:147
  212.3 2.4 collective-permute-start.1
  216.7 117.3 %copy-start.3 = (f32[512]{0:T(512)S(1)}, f32[512]{0:T(512)}, u32[]{:S(2)}) copy-start(f32[512]{0:T(512)} %param.27) | copy-start | bytes 6148
  216.8 3.3 collective-permute-start
  220.2 6.8 %collective-permute-start = (bf16[8,64,128]{2,1,0:T(8,128)(2,1)S(1)}, bf16[8,64,128]{2,1,0:T(8,128)(2,1)S(1)}, u32[]{:S(2)}, u32[]{:S(2)}) collective-permute-start(bf16[8,64,128]{2,1,0:T(8,128)(2,1)S(1)} %fusion.56), channel_id=1, source_target_pairs={{0,16},{16,32},{32,48},{48,64},{64,80},{80,96},{96,112},{112,128},... | collective-permute-start | bytes 393224 | tf_op jit(solution)/shard_map/while/body/eval_jaxpr/ppermute | solution.py:19
  227.1 8.9 %collective-permute-start = (bf16[8,64,128]{2,1,0:T(8,128)(2,1)S(1)}, bf16[8,64,128]{2,1,0:T(8,128)(2,1)S(1)}, u32[]{:S(2)}, u32[]{:S(2)}) collective-permute-start(bf16[8,64,128]{2,1,0:T(8,128)(2,1)S(1)} %fusion.56), channel_id=1, source_target_pairs={{0,16},{16,32},{32,48},{48,64},{64,80},{80,96},{96,112},{112,128},... | collective-permute-start | bytes 393224 | tf_op jit(solution)/shard_map/while/body/eval_jaxpr/ppermute | solution.py:19
  236.1 9.1 %collective-permute-start = (bf16[8,64,128]{2,1,0:T(8,128)(2,1)S(1)}, bf16[8,64,128]{2,1,0:T(8,128)(2,1)S(1)}, u32[]{:S(2)}, u32[]{:S(2)}) collective-permute-start(bf16[8,64,128]{2,1,0:T(8,128)(2,1)S(1)} %fusion.56), channel_id=1, source_target_pairs={{0,16},{16,32},{32,48},{48,64},{64,80},{80,96},{96,112},{112,128},... | collective-permute-start | bytes 393224 | tf_op jit(solution)/shard_map/while/body/eval_jaxpr/ppermute | solution.py:19
  245.3 9.1 %collective-permute-start = (bf16[8,64,128]{2,1,0:T(8,128)(2,1)S(1)}, bf16[8,64,128]{2,1,0:T(8,128)(2,1)S(1)}, u32[]{:S(2)}, u32[]{:S(2)}) collective-permute-start(bf16[8,64,128]{2,1,0:T(8,128)(2,1)S(1)} %fusion.56), channel_id=1, source_target_pairs={{0,16},{16,32},{32,48},{48,64},{64,80},{80,96},{96,112},{112,128},... | collective-permute-start | bytes 393224 | tf_op jit(solution)/shard_map/while/body/eval_jaxpr/ppermute | solution.py:19
  254.5 9.1 %collective-permute-start = (bf16[8,64,128]{2,1,0:T(8,128)(2,1)S(1)}, bf16[8,64,128]{2,1,0:T(8,128)(2,1)S(1)}, u32[]{:S(2)}, u32[]{:S(2)}) collective-permute-start(bf16[8,64,128]{2,1,0:T(8,128)(2,1)S(1)} %fusion.56), channel_id=1, source_target_pairs={{0,16},{16,32},{32,48},{48,64},{64,80},{80,96},{96,112},{112,128},... | collective-permute-start | bytes 393224 | tf_op jit(solution)/shard_map/while/body/eval_jaxpr/ppermute | solution.py:19
  263.8 8.6 %collective-permute-start = (bf16[8,64,128]{2,1,0:T(8,128)(2,1)S(1)}, bf16[8,64,128]{2,1,0:T(8,128)(2,1)S(1)}, u32[]{:S(2)}, u32[]{:S(2)}) collective-permute-start(bf16[8,64,128]{2,1,0:T(8,128)(2,1)S(1)} %fusion.56), channel_id=1, source_target_pairs={{0,16},{16,32},{32,48},{48,64},{64,80},{80,96},{96,112},{112,128},... | collective-permute-start | bytes 393224 | tf_op jit(solution)/shard_map/while/body/eval_jaxpr/ppermute | solution.py:19
  272.6 6.3 %collective-permute-start = (bf16[8,64,128]{2,1,0:T(8,128)(2,1)S(1)}, bf16[8,64,128]{2,1,0:T(8,128)(2,1)S(1)}, u32[]{:S(2)}, u32[]{:S(2)}) collective-permute-start(bf16[8,64,128]{2,1,0:T(8,128)(2,1)S(1)} %fusion.56), channel_id=1, source_target_pairs={{0,16},{16,32},{32,48},{48,64},{64,80},{80,96},{96,112},{112,128},... | collective-permute-start | bytes 393224 | tf_op jit(solution)/shard_map/while/body/eval_jaxpr/ppermute | solution.py:19
  279.0 6.3 %collective-permute-start = (bf16[8,64,128]{2,1,0:T(8,128)(2,1)S(1)}, bf16[8,64,128]{2,1,0:T(8,128)(2,1)S(1)}, u32[]{:S(2)}, u32[]{:S(2)}) collective-permute-start(bf16[8,64,128]{2,1,0:T(8,128)(2,1)S(1)} %fusion.56), channel_id=1, source_target_pairs={{0,16},{16,32},{32,48},{48,64},{64,80},{80,96},{96,112},{112,128},... | collective-permute-start | bytes 393224 | tf_op jit(solution)/shard_map/while/body/eval_jaxpr/ppermute | solution.py:19
  285.5 6.3 %collective-permute-start = (bf16[8,64,128]{2,1,0:T(8,128)(2,1)S(1)}, bf16[8,64,128]{2,1,0:T(8,128)(2,1)S(1)}, u32[]{:S(2)}, u32[]{:S(2)}) collective-permute-start(bf16[8,64,128]{2,1,0:T(8,128)(2,1)S(1)} %fusion.56), channel_id=1, source_target_pairs={{0,16},{16,32},{32,48},{48,64},{64,80},{80,96},{96,112},{112,128},... | collective-permute-start | bytes 393224 | tf_op jit(solution)/shard_map/while/body/eval_jaxpr/ppermute | solution.py:19
  291.9 6.3 %collective-permute-start = (bf16[8,64,128]{2,1,0:T(8,128)(2,1)S(1)}, bf16[8,64,128]{2,1,0:T(8,128)(2,1)S(1)}, u32[]{:S(2)}, u32[]{:S(2)}) collective-permute-start(bf16[8,64,128]{2,1,0:T(8,128)(2,1)S(1)} %fusion.56), channel_id=1, source_target_pairs={{0,16},{16,32},{32,48},{48,64},{64,80},{80,96},{96,112},{112,128},... | collective-permute-start | bytes 393224 | tf_op jit(solution)/shard_map/while/body/eval_jaxpr/ppermute | solution.py:19
  298.3 6.3 %collective-permute-start = (bf16[8,64,128]{2,1,0:T(8,128)(2,1)S(1)}, bf16[8,64,128]{2,1,0:T(8,128)(2,1)S(1)}, u32[]{:S(2)}, u32[]{:S(2)}) collective-permute-start(bf16[8,64,128]{2,1,0:T(8,128)(2,1)S(1)} %fusion.56), channel_id=1, source_target_pairs={{0,16},{16,32},{32,48},{48,64},{64,80},{80,96},{96,112},{112,128},... | collective-permute-start | bytes 393224 | tf_op jit(solution)/shard_map/while/body/eval_jaxpr/ppermute | solution.py:19
  304.7 6.3 %collective-permute-start = (bf16[8,64,128]{2,1,0:T(8,128)(2,1)S(1)}, bf16[8,64,128]{2,1,0:T(8,128)(2,1)S(1)}, u32[]{:S(2)}, u32[]{:S(2)}) collective-permute-start(bf16[8,64,128]{2,1,0:T(8,128)(2,1)S(1)} %fusion.56), channel_id=1, source_target_pairs={{0,16},{16,32},{32,48},{48,64},{64,80},{80,96},{96,112},{112,128},... | collective-permute-start | bytes 393224 | tf_op jit(solution)/shard_map/while/body/eval_jaxpr/ppermute | solution.py:19
  311.2 6.3 %collective-permute-start = (bf16[8,64,128]{2,1,0:T(8,128)(2,1)S(1)}, bf16[8,64,128]{2,1,0:T(8,128)(2,1)S(1)}, u32[]{:S(2)}, u32[]{:S(2)}) collective-permute-start(bf16[8,64,128]{2,1,0:T(8,128)(2,1)S(1)} %fusion.56), channel_id=1, source_target_pairs={{0,16},{16,32},{32,48},{48,64},{64,80},{80,96},{96,112},{112,128},... | collective-permute-start | bytes 393224 | tf_op jit(solution)/shard_map/while/body/eval_jaxpr/ppermute | solution.py:19
  317.6 6.3 %collective-permute-start = (bf16[8,64,128]{2,1,0:T(8,128)(2,1)S(1)}, bf16[8,64,128]{2,1,0:T(8,128)(2,1)S(1)}, u32[]{:S(2)}, u32[]{:S(2)}) collective-permute-start(bf16[8,64,128]{2,1,0:T(8,128)(2,1)S(1)} %fusion.56), channel_id=1, source_target_pairs={{0,16},{16,32},{32,48},{48,64},{64,80},{80,96},{96,112},{112,128},... | collective-permute-start | bytes 393224 | tf_op jit(solution)/shard_map/while/body/eval_jaxpr/ppermute | solution.py:19
  325.3 3.6 collective-permute-start.2
  328.9 5.0 %collective-permute-start.3 = (f32[128]{0:T(128)S(1)}, f32[128]{0:T(128)S(1)}, u32[]{:S(2)}, u32[]{:S(2)}) collective-permute-start(f32[128]{0:T(128)S(1)} %add.99), channel_id=1, source_target_pairs={{0,2},{2,0},{1,3},{3,1},{4,6},{6,4},{5,7},{7,5},{8,10},{10,8},{9,1... | collective-permute-start | bytes 1544 | tf_op jit(solution)/shard_map/ppermute | solution.py:29
  (9 other events, 376.0 us)
Sparse Core Ops, SparseCore 0:
  9.8 51.9 all-gather.2
  137.2 72.7 reduce-scatter.2
  211.8 59.6 all-gather.4
  340.3 102.9 reduce-scatter.4
where the time goes:
time: 453 us; the launch traced here: 451 us
  waiting for transfers between devices  292 us (64%)
  starting transfers between devices  104 us (23%)
  other arithmetic  17.2 us (4%)
  matrix products  16.4 us (4%)
  between operations  14.7 us (3%)
  local copies, waits for them, and re-layouts  6.96 us (2%)
    reduce_scatter x1, waiting for transfers between devices, local(): lax.psum_scatter(terms.astype(jnp.bfloat16), 'fsdp', scatter_dimension=1,...  103 us
    ppermute x16, starting transfers between devices, from_behind(): lax.ppermute(value, axis, [(source, source + steps) for source in range(l...  91.9 us
    reduce_scatter x1, waiting for transfers between devices, local(): lax.psum_scatter(jnp.dot(spread, stacked, preferred_element_type=jnp.floa...  67.5 us
    all_gather x1, waiting for transfers between devices, local(): gathered = lax.all_gather(tokens, 'fsdp', axis=1, tiled=True)  53.5 us
    all_to_all x1, waiting for transfers between devices, local(): lax.all_to_all(normed, 'seq', split_axis=1, concat_axis=0, tiled=True)  48.3 us
    ppermute x16, waiting for transfers between devices, from_behind(): lax.ppermute(value, axis, [(source, source + steps) for source in range(l...  14.6 us
  transfers between devices with their start and end apart: 23, of which 22 were waited for; matrix products, arithmetic and copies ran while one was open for 3% of the time, Pallas kernels for 0%

commit v1 on v0

v1 whole, which is shorter than its diff:
```python
import jax
import jax.numpy as jnp
from jax import lax
from jax.experimental import pallas as pl
from jax.experimental.pallas import tpu as pltpu
from jax.sharding import PartitionSpec as P

N = 128
EPSILON = 1e-05
PRECISE = lax.Precision.HIGHEST
MESH = pl.DeviceIdType.MESH
F32 = jnp.float32
BF16 = jnp.bfloat16
WIDE = 640
STEP0 = 32
SQ = 36
SENDS = 200


def dot(a, b, precision=None):
    return jnp.dot(a, b, preferred_element_type=F32, precision=precision)


def body(
    tok, gain, gate_w, value_w, extra_w, conv_v, conv_s, mix_gain, out_w,
    bias, rate, skip, docs,
    out,
    X, W, WS, PS, SL, SS, RL, RS, R, HS, HR, EXT, BC, ST, SR, SO, SI, GS, SQB, GZ, T, Q, A1, B1, C1, RA1, RB1, RC1,
    A2, B2, C2, RA2, RB2, RC2, FO, FR,
    sem_send, sem_a, sem_y, sem_x, sem_s, sem_w, sem_l, sem_sh, sem_h, sem_bc, sem_st, sem_in, sem_sq, sem_g, sem_gs,
    sem_1, sem_2, sem_f, sem_loc,
):
    s = lax.axis_index("seq")
    f = lax.axis_index("fsdp")
    z, c = lax.div(s, 2), lax.rem(s, 2)
    x, y = lax.div(f, 4), lax.rem(f, 4)
    sg = 1 - 2 * c

    def m4(v):
        return lax.rem(v + 8, 4)

    def m8(v):
        return lax.rem(v + 16, 8)

    def dev(z_=z, c_=c, x_=x, y_=y):
        return (2 * z_ + c_, 4 * x_ + y_)

    sibling = dev(c_=1 - c)
    started = []

    def send(src, dst, sem, to):
        copy = pltpu.make_async_remote_copy(
            src_ref=src, dst_ref=dst, send_sem=sem_send.at[len(started)], recv_sem=sem,
            device_id=to, device_id_type=MESH,
        )
        copy.start()
        started.append((copy, None))

    def arrived(dst, sem):
        pltpu.make_async_remote_copy(
            src_ref=dst, dst_ref=dst, send_sem=sem_send.at[0], recv_sem=sem,
            device_id=sibling, device_id_type=MESH,
        ).wait_recv()

    def send_or_keep(own, src, dst, sem, to):
        copy = pltpu.make_async_remote_copy(
            src_ref=src, dst_ref=dst, send_sem=sem_send.at[len(started)], recv_sem=sem,
            device_id=to, device_id_type=MESH,
        )
        away = jnp.logical_not(own)

        @pl.when(away)
        def _():
            copy.start()

        @pl.when(own)
        def _():
            pltpu.make_async_copy(src, dst, sem).start()

        started.append((copy, away))

    for i in range(8):
        px, py = 2 * c + i // 4, i % 4
        own = (f == s) & (f == 8 * c + i)
        send_or_keep(
            own, tok.at[pl.ds(16 * i, 16)], X.at[lax.rem(f, 2), px, py, z], sem_a.at[z], (f, 4 * px + py)
        )

    gain_col = jnp.transpose(
        jnp.broadcast_to(gain[0:1, pl.ds(pl.multiple_of(512 * s, 512), 512)], (128, 512))
    )[:, 0:1]

    def rows_of(half, ref):
        cols = pl.ds(pl.multiple_of(256 * half, 256), 256)
        ref[:, 0:256] = (gate_w[:, cols].astype(F32) * gain_col).astype(BF16)
        ref[:, 256:512] = (value_w[:, cols].astype(F32) * gain_col).astype(BF16)
        ref[:, 512:640] = (extra_w[half].astype(F32) * gain_col).astype(BF16)

    rows_of(1 - c, WS)
    send(WS, W.at[c], sem_w, sibling)
    rows_of(c, W.at[c])

    lane8 = lax.broadcasted_iota(jnp.int32, (8, 128), 1)
    starts = jnp.full((8, 128), 1 << 20, jnp.int32)
    total = jnp.int32(0)
    for i in range(32):
        starts = jnp.where(lane8 == i, total, starts)
        total = total + docs[i]
    starts = starts.astype(F32)[0:1]
    first = (256 * z).astype(F32)
    t_wide = first + lax.broadcasted_iota(jnp.int32, (256, 128), 0).astype(F32)
    start_of = jnp.max(jnp.where(starts <= t_wide, starts, 0.0), axis=1, keepdims=True)
    t_col = t_wide[:, 0:1]
    into = t_col - start_of
    row8 = lane8
    bias_row = jnp.zeros((8, 128), F32)
    rate_row = jnp.zeros((8, 128), F32)
    lane_256 = lax.broadcasted_iota(jnp.int32, (8, 256), 1)
    skip_row = jnp.zeros((8, 256), F32)
    for i in range(4):
        bias_row = jnp.where(row8 == STEP0 + i, bias[4 * c + i], bias_row)
        rate_row = jnp.where(row8 == STEP0 + i, rate[4 * c + i], rate_row)
        skip_row = jnp.where(lax.div(lane_256, 64) == i, skip[4 * c + i], skip_row)
    bias_row, rate_row, skip_row = bias_row[0:1], rate_row[0:1], skip_row[0:1]

    for zt in range(8):
        arrived(X.at[c, x, y, zt], sem_a.at[zt])
    mine = X.at[c, x, y]
    send(mine, mine, sem_y.at[y], dev(y_=m4(y + 1)))
    send(mine, mine, sem_y.at[y], dev(y_=m4(y - 1)))
    near = X.at[c, x, m4(y - sg)]
    arrived(near, sem_y.at[m4(y - sg)])
    send(near, near, sem_y.at[m4(y - sg)], dev(y_=m4(y + sg)))
    arrived(X.at[c, x, m4(y + sg)], sem_y.at[m4(y + sg)])
    arrived(X.at[c, x, m4(y + 2)], sem_y.at[m4(y + 2)])
    mine = X.at[c, x]
    send(mine, mine, sem_s.at[x], sibling)
    send(mine, mine, sem_x.at[x], dev(x_=m4(x + 1)))
    send(mine, mine, sem_x.at[x], dev(x_=m4(x - 1)))
    arrived(W.at[1 - c], sem_w)

    lane_e = lax.broadcasted_iota(jnp.int32, (256, 128), 1)

    def product(g, xg):
        other = X.at[1 - c, xg]
        arrived(other, sem_s.at[xg])

        def half(i, carry):
            a = X[0, xg, pl.ds(2 * i, 2)].reshape(256, 512)
            b = X[1, xg, pl.ds(2 * i, 2)].reshape(256, 512)
            p = dot(a, W[0]) + dot(b, W[1])
            a, b = a.astype(F32), b.astype(F32)
            squares = jnp.sum(a * a + b * b, axis=1, keepdims=True)
            PS[g, pl.ds(2 * i, 2), :, :, 0:512] = p[:, 0:512].reshape(2, 8, 16, 512)
            PS[g, pl.ds(2 * i, 2), :, :, 512:640] = (
                p[:, 512:640] + jnp.where(lane_e == SQ, squares, 0.0)
            ).reshape(2, 8, 16, 128)
            return carry

        lax.fori_loop(0, 2, half, 0)

    def hop(g, k):
        if k:
            arrived(RL.at[g, k - 1], sem_l.at[g, k - 1])
        long = PS[g, :, m8(z + (4 - k) * sg)]
        SL[g, k] = (long + RL[g, k - 1].astype(F32) if k else long).astype(BF16)
        send(SL.at[g, k], RL.at[g, k], sem_l.at[g, k], dev(z_=m8(z + sg)))
        if k < 3:
            if k:
                arrived(RS.at[g, k - 1], sem_sh.at[g, k - 1])
            short = PS[g, :, m8(z - (3 - k) * sg)]
            SS[g, k] = (short + RS[g, k - 1].astype(F32) if k else short).astype(BF16)
            send(SS.at[g, k], RS.at[g, k], sem_sh.at[g, k], dev(z_=m8(z - sg)))

    def last(g, xg):
        arrived(RL.at[g, 3], sem_l.at[g, 3])
        arrived(RS.at[g, 2], sem_sh.at[g, 2])
        R[xg] = PS[g, :, z] + RL[g, 3].astype(F32) + RS[g, 2].astype(F32)

    groups = [x, m4(x - sg), m4(x + sg), m4(x + 2)]

    def came(j):
        got = X.at[c, groups[j]]
        arrived(got, sem_x.at[groups[j]])
        if j == 1:
            send(got, got, sem_x.at[groups[j]], dev(x_=m4(x + sg)))
        send(got, got, sem_s.at[groups[j]], sibling)

    product(0, groups[0])
    for k in range(4):
        hop(0, k)
    came(1)
    came(2)
    product(1, groups[1])
    hop(1, 0)
    last(0, groups[0])
    product(2, groups[2])
    hop(2, 0)
    hop(1, 1)
    hop(2, 1)
    hop(1, 2)
    hop(2, 2)
    hop(1, 3)
    came(3)
    product(3, groups[3])
    hop(3, 0)
    hop(2, 3)
    last(1, groups[1])
    hop(3, 1)
    last(2, groups[2])
    hop(3, 2)
    hop(3, 3)
    last(3, groups[3])

    scale = lax.rsqrt(R[:, :, :, 512:640].reshape(256, 128)[:, SQ : SQ + 1] * (1.0 / 8192) + EPSILON)
    raw = (R[:, :, :, 256:640].reshape(256, 384) * scale).astype(BF16)
    HS[...] = raw[240:256]
    send(HS, HR, sem_h, dev(z_=m8(z + 1)))
    EXT[16:272] = raw.astype(F32)
    gate = R[:, :, :, 0:256].reshape(256, 256) * scale
    GS[...] = gate * jax.nn.sigmoid(gate)

    raw_step = R[:, :, :, 512:640].reshape(256, 128) * scale + bias_row
    step = jnp.maximum(raw_step, 0.0) + jnp.log1p(jnp.exp(-jnp.abs(raw_step)))
    log_decay = -rate_row * step
    order_r = lax.broadcasted_iota(jnp.int32, (256, 256), 0)
    order_c = lax.broadcasted_iota(jnp.int32, (256, 256), 1)
    cum = dot((order_r >= order_c).astype(F32), log_decay, PRECISE)
    cum_rows = jnp.transpose(cum)
    end = cum[255:256]
    causal = (order_r >= order_c) & (first + order_c.astype(F32) >= start_of)
    start_last = start_of[255:256]
    low = lax.broadcasted_iota(jnp.int32, (1, 128), 1) < 64

    def expand(a):
        return jnp.concatenate(
            [
                jnp.where(low, a[:, STEP0 + 2 * i : STEP0 + 2 * i + 1], a[:, STEP0 + 2 * i + 1 : STEP0 + 2 * i + 2])
                for i in range(2)
            ],
            axis=1,
        )

    step_wide = expand(step)
    tail = expand(jnp.where(t_col >= start_last, jnp.exp(end - cum), 0.0))
    carried = expand(jnp.where(start_of < first, jnp.exp(cum), 0.0))
    passing = expand(jnp.where(start_last < first, jnp.exp(end), 0.0))

    arrived(HR, sem_h)
    EXT[0:16] = HR[...].astype(F32)

    def conv(lo, width, taps):
        acc = jnp.zeros((256, width), F32)
        for k in range(4):
            acc = acc + jnp.where(into >= 3 - k, EXT[13 + k : 269 + k, lo : lo + width], 0.0) * taps[k]
        return acc * jax.nn.sigmoid(acc)

    turn = lax.rem(128 - 32 * y, 128)
    maps_cols = pl.ds(pl.multiple_of(128 * c, 128), 128)
    group_row = lax.broadcasted_iota(jnp.int32, (4, 128), 0) == x
    taps_s = [
        pltpu.roll(
            jnp.broadcast_to(
                jnp.sum(jnp.where(group_row, conv_s[k, :, maps_cols], 0.0), axis=0, keepdims=True), (8, 128)
            ),
            turn,
            1,
        )[0:1]
        for k in range(4)
    ]
    maps = jnp.transpose(conv(256, 128, taps_s))[0:32].astype(BF16)
    BC[c, y] = maps
    peers = [(dc, dy) for dc in range(2) for dy in range(4) if (dc, dy) != (0, 0)]
    for dc, dy in peers:
        to_c = lax.rem(c + dc, 2)
        send(BC.at[c, y], BC.at[c, y], sem_bc.at[4 * c + y], dev(c_=to_c, y_=m4(y + dy)))

    own_cols = pl.ds(pl.multiple_of(256 * c, 256), 256)
    inputs = conv(0, 256, [conv_v[k : k + 1, own_cols] for k in range(4)]).astype(BF16).astype(F32)
    stepped = inputs * step_wide
    to_end = (stepped * tail).astype(BF16)
    stepped = stepped.astype(BF16)

    for dc, dy in peers:
        pc, py = lax.rem(c + dc, 2), m4(y + dy)
        arrived(BC.at[pc, py], sem_bc.at[4 * pc + py])
    b_rows = BC[0].reshape(128, 256)
    c_cols = jnp.transpose(BC[1].reshape(128, 256).astype(F32)).astype(BF16)

    state = dot(b_rows, to_end).astype(BF16)
    ST[:, 0:16] = state.reshape(8, 16, 256)
    ST[:, 16:32] = jnp.broadcast_to(passing.astype(BF16)[None], (8, 16, 256))
    for o in range(1, 8):
        k = m8(z + o)
        send(ST.at[k], SR.at[z], sem_st.at[z], dev(z_=k))
    SR[z] = ST[z]

    scores = dot(c_cols, b_rows)
    parts = []
    for i in range(4):
        gaps = cum[:, STEP0 + i : STEP0 + i + 1] - cum_rows[STEP0 + i : STEP0 + i + 1, :]
        mixing = (jnp.exp(jnp.where(causal, gaps, -1e30)) * scores).astype(BF16)
        parts.append(dot(mixing, stepped[:, 128 * (i // 2) : 128 * (i // 2) + 128]))
    intra = jnp.concatenate([jnp.where(low, parts[0], parts[1]), jnp.where(low, parts[2], parts[3])], axis=1)
    partly = intra + skip_row * inputs

    for o in range(1, 8):
        k = m8(z + o)
        arrived(SR.at[k], sem_st.at[k])
    incoming = jnp.zeros((16, 256), F32)
    for i in range(8):
        SO[i] = incoming.astype(BF16)
        incoming = SR[i, 16:32].astype(F32) * incoming + SR[i, 0:16].astype(F32)
    for o in range(1, 8):
        k = m8(z + o)
        send(SO.at[k], SI.at[z], sem_in.at[z], dev(z_=k))
    SI[z] = SO[z]
    for o in range(1, 8):
        k = m8(z + o)
        arrived(SI.at[k], sem_in.at[k])
    outputs = partly + dot(c_cols, SI[...].reshape(128, 256)) * carried
    gated = outputs * GS[...]

    own_sq = 2 * y + c
    SQB[own_sq] = lax.dot_general(
        jnp.ones((8, 256), F32), gated * gated, (((1,), (1,)), ((), ())), preferred_element_type=F32, precision=PRECISE
    )
    for dc, dy in peers:
        send(SQB.at[own_sq], SQB.at[own_sq], sem_sq.at[own_sq], dev(c_=lax.rem(c + dc, 2), y_=m4(y + dy)))
    for dc, dy in peers:
        k = 2 * m4(y + dy) + lax.rem(c + dc, 2)
        arrived(SQB.at[k], sem_sq.at[k])
    squares = jnp.sum(SQB[...], axis=0)
    norm = lax.rsqrt(squares * (1.0 / 2048) + EPSILON)
    norm = jnp.transpose(jnp.concatenate([norm] * 16, axis=0))[:, 0:1]
    GZ[c, z] = (gated * norm * mix_gain[0:1, own_cols]).astype(BF16)

    order = [z]
    for k in range(1, 4):
        order += [m8(z - k * sg), m8(z + k * sg)]
    order.append(m8(z + 4))
    block = GZ.at[c, z]
    send(block, block, sem_g.at[z], dev(z_=m8(z + sg)))
    send(block, block, sem_g.at[z], dev(z_=m8(z - sg)))
    send(block, block, sem_gs.at[z], sibling)

    def pass_on(o):
        zt = order[o]
        got = GZ.at[c, zt]
        arrived(got, sem_g.at[zt])
        if o in (1, 3, 5):
            send(got, got, sem_g.at[zt], dev(z_=m8(z + sg)))
        if o in (2, 4):
            send(got, got, sem_g.at[zt], dev(z_=m8(z - sg)))
        send(got, got, sem_gs.at[zt], sibling)

    def take(o):
        zt = order[o]
        if o % 2 == 1:
            pass_on(o)
            if o < 7:
                pass_on(o + 1)
        arrived(GZ.at[1 - c, zt], sem_gs.at[zt])
        T[o] = (dot(GZ[0, zt], out_w[0:256]) + dot(GZ[1, zt], out_w[256:512])).reshape(4, 4, 16, 512)

    def along(o, level):
        over_x = (o % 2 == 0) == (level == 1)
        p = x if over_x else y

        def to(q):
            return dev(x_=q) if over_x else dev(y_=q)

        return p, to

    def quarter(o, q):
        return T[o, q] if o % 2 == 0 else T[o, :, q]

    def first_out(o):
        p, to = along(o, 1)
        A1[o] = quarter(o, m4(p + 2)).astype(BF16)
        send(A1.at[o], RA1.at[o], sem_1.at[o, 0], to(m4(p + sg)))
        B1[o] = quarter(o, m4(p - sg)).astype(BF16)
        send(B1.at[o], RB1.at[o], sem_1.at[o, 1], to(m4(p - sg)))

    def first_relay(o):
        p, to = along(o, 1)
        arrived(RA1.at[o], sem_1.at[o, 0])
        C1[o] = (quarter(o, m4(p + sg)) + RA1[o].astype(F32)).astype(BF16)
        send(C1.at[o], RC1.at[o], sem_1.at[o, 2], to(m4(p + sg)))

    def second_out(o):
        p, _ = along(o, 1)
        arrived(RB1.at[o], sem_1.at[o, 1])
        arrived(RC1.at[o], sem_1.at[o, 2])
        Q[o] = quarter(o, p) + RB1[o].astype(F32) + RC1[o].astype(F32)
        p, to = along(o, 2)
        A2[o] = Q[o, m4(p + 2)].astype(BF16)
        send(A2.at[o], RA2.at[o], sem_2.at[o, 0], to(m4(p + sg)))
        B2[o] = Q[o, m4(p - sg)].astype(BF16)
        send(B2.at[o], RB2.at[o], sem_2.at[o, 1], to(m4(p - sg)))

    def second_relay(o):
        p, to = along(o, 2)
        arrived(RA2.at[o], sem_2.at[o, 0])
        C2[o] = (Q[o, m4(p + sg)] + RA2[o].astype(F32)).astype(BF16)
        send(C2.at[o], RC2.at[o], sem_2.at[o, 2], to(m4(p + sg)))

    block_at = f
    row_block = lax.rem(block_at, 8)
    to_core = lax.div(block_at, 8)

    def finish(o):
        p, _ = along(o, 2)
        arrived(RB2.at[o], sem_2.at[o, 1])
        arrived(RC2.at[o], sem_2.at[o, 2])
        FO[o] = (Q[o, p] + RB2[o].astype(F32) + RC2[o].astype(F32)).astype(BF16)
        to = (2 * order[o] + to_core, s)
        own = (to[0] == s) & (s == f) if o == 0 else None
        if own is None:
            send(FO.at[o], FR.at[row_block], sem_f.at[row_block], to)
        else:
            send_or_keep(own, FO.at[o], FR.at[row_block], sem_f.at[row_block], to)

    for tick in range(8 + 4):
        if tick < 8:
            take(tick)
            first_out(tick)
        if 0 <= tick - 1 < 8:
            first_relay(tick - 1)
        if 0 <= tick - 2 < 8:
            second_out(tick - 2)
        if 0 <= tick - 3 < 8:
            second_relay(tick - 3)
        if 0 <= tick - 4 < 8:
            finish(tick - 4)

    for i in range(8):
        arrived(FR.at[i], sem_f.at[i])
    out[...] = (tok[...].astype(F32) + FR[...].reshape(128, 512).astype(F32)).astype(BF16)

    for copy, away in started:
        if away is None:
            copy.wait_send()
        else:

            @pl.when(away)
            def _(copy=copy):
                copy.wait_send()

    assert len(started) <= SENDS


def local(
    tokens, norm_gain, gate_proj, value_proj, step_proj, state_proj, conv_value, conv_state, step_bias, decay_rate,
    skip_gain, mix_gain, out_proj, doc_lengths,
):
    f = lax.axis_index("fsdp")
    x, y = f // 4, f % 4
    rows = state_proj.shape[0]
    halves = []
    for core in range(2):
        maps = lax.dynamic_slice(state_proj, (0, x, 128 * core + 32 * y), (rows, 1, 32))[:, 0]
        halves.append(
            jnp.concatenate([maps, step_proj[:, 4 * core : 4 * core + 4], jnp.zeros((rows, 92), BF16)], axis=1)
        )
    extra = jnp.stack(halves)
    vmem = pl.BlockSpec(memory_space=pltpu.VMEM)
    smem = pl.BlockSpec(memory_space=pltpu.SMEM)

    def buf(*shape, dtype=BF16):
        return pltpu.VMEM(shape, dtype)

    def dma(*shape):
        return pltpu.SemaphoreType.DMA(shape)

    return pl.pallas_call(
        body,
        out_shape=jax.ShapeDtypeStruct((128, 512), BF16),
        in_specs=[vmem] * 9 + [smem] * 4,
        out_specs=vmem,
        scratch_shapes=[
            buf(2, 4, 4, 8, 16, 512),
            buf(2, 512, WIDE),
            buf(512, WIDE),
            buf(4, 4, 8, 16, WIDE, dtype=F32),
            buf(4, 4, 4, 16, WIDE),
            buf(4, 3, 4, 16, WIDE),
            buf(4, 4, 4, 16, WIDE),
            buf(4, 3, 4, 16, WIDE),
            buf(4, 4, 16, WIDE, dtype=F32),
            buf(16, 384),
            buf(16, 384),
            buf(272, 384, dtype=F32),
            buf(2, 4, 32, 256),
            buf(8, 32, 256),
            buf(8, 32, 256),
            buf(8, 16, 256),
            buf(8, 16, 256),
            buf(256, 256, dtype=F32),
            buf(8, 8, 256, dtype=F32),
            buf(2, 8, 256, 256),
            buf(8, 4, 4, 16, 512, dtype=F32),
            buf(8, 4, 16, 512, dtype=F32),
        ]
        + [buf(8, 4, 16, 512)] * 6
        + [buf(8, 16, 512)] * 6
        + [buf(8, 16, 512)] * 2
        + [
            dma(SENDS), dma(8), dma(4), dma(4), dma(4), dma(), dma(4, 4), dma(4, 3), dma(), dma(8), dma(8), dma(8),
            dma(8), dma(8), dma(8), dma(8, 3), dma(8, 3), dma(8), dma(),
        ],
        compiler_params=pltpu.CompilerParams(has_side_effects=True, vmem_limit_bytes=56 * 2**20),
        name="mixer",
    )(
        tokens, norm_gain.reshape(1, -1), gate_proj, value_proj, extra, conv_value, conv_state, mix_gain.reshape(1, -1),
        out_proj, step_bias, decay_rate, skip_gain, doc_lengths,
    )


def solution(mesh):
    return jax.shard_map(
        local,
        mesh=mesh,
        in_specs=(
            P("seq", "fsdp"), P(), P("seq", "fsdp"), P("seq", "fsdp"), P("seq", "fsdp"), P("seq", None, None),
            P(None, "fsdp"), P(), P("fsdp"), P("fsdp"), P("fsdp"), P("fsdp"), P("fsdp", "seq"), P(),
        ),
        out_specs=P("seq", "fsdp"),
        check_vma=False,
    )
```

time: 453 us -> 164 us (0.36)
  waiting for transfers between devices: 292 us -> 0 us
  Pallas kernels: 0 us -> 158 us
  starting transfers between devices: 104 us -> 0 us
  matrix products: 16.4 us -> 0 us
  other arithmetic: 17.2 us -> 0.88 us
  between operations: 14.7 us -> 0.05 us
    reduce_scatter x2 -> x0, waiting for transfers between devices: 171 us -> none  [the longest x1 103 us: local(): lax.psum_scatter(terms.astype(jnp.bfloat16), 'fsdp', scatter_dimension=1,...]
    pallas_call x0 -> x1, Pallas kernels: none -> 158 us  [local(): pl.pallas_call(body, out_shape=jax.ShapeDtypeStruct((128, 512), BF16), in...]
    ppermute x18 -> x0, starting transfers between devices: 96.5 us -> none  [the longest x16 91.9 us: from_behind(): lax.ppermute(value, axis, [(source, source + steps) for source in range(l...]
    all_gather x2 -> x0, waiting for transfers between devices: 53.5 us -> none  [the longest x1 53.5 us: local(): gathered = lax.all_gather(tokens, 'fsdp', axis=1, tiled=True)]
    all_to_all x1 -> x0, waiting for transfers between devices: 48.3 us -> none  [local(): lax.all_to_all(normed, 'seq', split_axis=1, concat_axis=0, tiled=True)]
    ppermute x18 -> x0, waiting for transfers between devices: 18.6 us -> none  [the longest x16 14.6 us: from_behind(): lax.ppermute(value, axis, [(source, source + steps) for source in range(l...]
    dot_general x6 -> x0, matrix products: 16.4 us -> none  [the longest x1 8.76 us: local(): jnp.dot(spread, stacked, preferred_element_type=jnp.float32)]
    convert_element_type x33 -> x0, other arithmetic: 8.72 us -> none  [the longest x1 4.58 us: local(): normed = (as_float * lax.rsqrt(jnp.mean(as_float * as_float, axis=1, keep...]
  transfers between devices with their start and end apart: 23 -> 0, of which waited for: 22 -> 0; matrix products, arithmetic and copies ran while one was open for 3% -> 0% of each run, Pallas kernels for 0% -> 0%
where the time goes in v1:
time: 164 us
  Pallas kernels  158 us (96%)
  local copies, waits for them, and re-layouts  4.75 us (3%)
    pallas_call x1, Pallas kernels, local(): pl.pallas_call(body, out_shape=jax.ShapeDtypeStruct((128, 512), BF16), in...  158 us

profile of v1, /device:TPU:4, one launch (start us, length us, event | category | flops | bytes accessed | tf_op | source)
XLA Modules:
  0.0 163.9 jit_solution(10716666726300812722)
XLA Ops:
  0.0 2.1 %constant_dynamic-slice_fusion.1 = (bf16[512,1,32]{2,1,0:T(2,128)(2,1)S(1)}, bf16[512,1,32]{2,1,0:T(2,128)(2,1)S(1)}) fusion(bf16[512,4,256]{2,1,0:T(4,128)(2,1)} %param.19, s32[]{:T(128)S(6)} %select_n.22, s32[]{:T(128)S(6)} %select_n.24, s32[]{:T(128)S(6)} %select_n.25), kind=kLoop, calls=%fused_computation.6 | loop fusion | bytes 131084 | tf_op jit(solution)/shard_map/dynamic_slice | solution.py:462
  2.1 0.0 copy-start
  2.1 0.6 copy-done
  2.8 0.2 copy.19
  2.9 0.2 copy.22
  3.1 0.1 pad.7.clone
  3.2 0.2 maximum_bitcast_fusion
  3.4 0.7 pad_maximum_fusion.extra_w
  4.1 158.2 %mixer.1 = bf16[128,512]{1,0:T(8,128)(2,1)} custom-call(bf16[128,512]{1,0:T(8,128)(2,1)} %tok.1, f32[1,8192]{1,0:T(1,128)} %bitcast.12, bf16[512,512]{1,0:T(8,128)(2,1)} %gate_w.1, bf16[512,512]{1,0:T(8,128)(2,1)} %value_w.1, bf16[2,512,128]{2,1,0:T(8,128)(2,1)} %pad_maximum_fusion.extra_w, f32[4,512]{1,0:T(4,128)} %conv_v.1, f32[4,4,256]{2,1,0:T(4,128)} %conv_s.1, ...), custom_call_target="tpu_custom_call" | custom-call | tf_op jit(solution)/shard_map/mixer/pallas_call | solution.py:476
  162.3 1.6 copy.30
  (3 shorter events, 0.0 us)
Async XLA Ops:
  2.1 0.7 copy-start

commit v2 on v1

--- a/solution.py
+++ b/solution.py
@@ -13,8 +13,8 @@
 BF16 = jnp.bfloat16
 WIDE = 640
 STEP0 = 32
-SQ = 36
-SENDS = 200
+SQ = 40
+SENDS = 260
 
 
 def dot(a, b, precision=None):
@@ -22,13 +22,14 @@
 
 
 def body(
-    tok, gain, gate_w, value_w, extra_w, conv_v, conv_s, mix_gain, out_w,
+    tok, gain, gate_w, value_w, maps_w, step_w, conv_v, conv_s, mix_gain, out_w,
     bias, rate, skip, docs,
     out,
-    X, W, WS, PS, SL, SS, RL, RS, R, HS, HR, EXT, BC, ST, SR, SO, SI, GS, SQB, GZ, T, Q, A1, B1, C1, RA1, RB1, RC1,
+    XI, X, WV, WG, SV, SG, PV, PG, S0L, S0S, R0L, R0S, S1L, S1S, R1L, R1S, S2L, S2S, R2L, R2S, S3L, S3S, R3L, R3S, RV, RG,
+    HS, HR, EXT, BC, ST, SR, SO, SI, SQB, NZ, GZ, T, Q, A1, B1, C1, RA1, RB1, RC1,
     A2, B2, C2, RA2, RB2, RC2, FO, FR,
-    sem_send, sem_a, sem_y, sem_x, sem_s, sem_w, sem_l, sem_sh, sem_h, sem_bc, sem_st, sem_in, sem_sq, sem_g, sem_gs,
-    sem_1, sem_2, sem_f, sem_loc,
+    sem_send, sem_i, sem_a, sem_y, sem_x, sem_s, sem_w, sem_l, sem_sh, sem_h, sem_bc, sem_st, sem_in, sem_sq, sem_nz,
+    sem_g, sem_gs, sem_1, sem_2, sem_f,
 ):
     s = lax.axis_index("seq")
     f = lax.axis_index("fsdp")
@@ -46,6 +47,7 @@
         return (2 * z_ + c_, 4 * x_ + y_)
 
     sibling = dev(c_=1 - c)
+    peers = [(dc, dy) for dc in range(2) for dy in range(4) if (dc, dy) != (0, 0)]
     started = []
 
     def send(src, dst, sem, to):
@@ -79,26 +81,74 @@
 
         started.append((copy, away))
 
+    def wrap_up():
+        for copy, away in started:
+            if away is None:
+                copy.wait_send()
+            else:
+
+                @pl.when(away)
+                def _(copy=copy):
+                    copy.wait_send()
+
+        assert len(started) <= SENDS
+
+    barrier = pltpu.get_barrier_semaphore()
+    own_leg = (lax.rem(f, 2) == c) & (lax.div(x, 2) == c)
+
+    def greet(to):
+        pl.semaphore_signal(barrier, inc=1, device_id=to, device_id_type=MESH)
+
     for i in range(8):
-        px, py = 2 * c + i // 4, i % 4
-        own = (f == s) & (f == 8 * c + i)
-        send_or_keep(
-            own, tok.at[pl.ds(16 * i, 16)], X.at[lax.rem(f, 2), px, py, z], sem_a.at[z], (f, 4 * px + py)
-        )
+        for to, at in (((2 * z + lax.rem(f, 2), 8 * c + i), 8 * c + i), ((2 * z + lax.div(x, 2), 2 * i + c), 2 * i + c)):
+
+            @pl.when(jnp.logical_not(own_leg & (f == at)))
+            def _(to=to):
+                greet(to)
+
+    for o in range(1, 8):
+        greet(dev(z_=m8(z + o)))
+    for dc, dy in peers:
+        greet(dev(c_=lax.rem(c + dc, 2), y_=m4(y + dy)))
+    greet(dev(x_=m4(x + 1)))
+    greet(dev(x_=m4(x - 1)))
 
     gain_col = jnp.transpose(
         jnp.broadcast_to(gain[0:1, pl.ds(pl.multiple_of(512 * s, 512), 512)], (128, 512))
     )[:, 0:1]
-
-    def rows_of(half, ref):
+    lane_w = lax.broadcasted_iota(jnp.int32, (512, 128), 1)
+    turn = lax.rem(128 - 32 * y, 128)
+
+    def rows_of(half, ref_v, ref_g):
         cols = pl.ds(pl.multiple_of(256 * half, 256), 256)
-        ref[:, 0:256] = (gate_w[:, cols].astype(F32) * gain_col).astype(BF16)
-        ref[:, 256:512] = (value_w[:, cols].astype(F32) * gain_col).astype(BF16)
-        ref[:, 512:640] = (extra_w[half].astype(F32) * gain_col).astype(BF16)
-
-    rows_of(1 - c, WS)
-    send(WS, W.at[c], sem_w, sibling)
-    rows_of(c, W.at[c])
+        ref_v[:, 0:256] = (value_w[:, cols].astype(F32) * gain_col).astype(BF16)
+        maps = pltpu.roll(maps_w[:, pl.ds(pl.multiple_of(128 * half, 128), 128)].astype(F32), turn, 1)
+        steps = pltpu.roll(step_w[...].astype(F32), lax.rem(8 - 4 * half, 8), 0)
+        steps = jnp.concatenate([jnp.zeros((32, 512), F32), steps, jnp.zeros((88, 512), F32)], axis=0)
+        extra = jnp.where(lane_w < 32, maps, 0.0) + jnp.transpose(steps)
+        ref_v[:, 256:384] = (extra * gain_col).astype(BF16)
+        ref_g[...] = (gate_w[:, cols].astype(F32) * gain_col).astype(BF16)
+
+    pl.semaphore_wait(barrier, 32 - 2 * own_leg.astype(jnp.int32))
+
+    for i in range(8):
+        send_or_keep(
+            own_leg & (f == 8 * c + i),
+            tok.at[pl.ds(16 * i, 16)], XI.at[lax.div(f, 2)], sem_i.at[lax.div(f, 2)],
+            (2 * z + lax.rem(f, 2), 8 * c + i),
+        )
+    rows_of(1 - c, SV, SG)
+    send(SV, WV.at[c], sem_w.at[0], sibling)
+    send(SG, WG.at[c], sem_w.at[1], sibling)
+    rows_of(c, WV.at[c], WG.at[c])
+    upper = lax.div(z, 4)
+    lead, trail = x + upper * (y - x), y + upper * (x - y)
+    for o in (4, 3, 5, 2, 6, 1, 7):
+        to = m8(z + o)
+        arrived(XI.at[to], sem_i.at[to])
+        send(XI.at[to], X.at[c, upper, lead, trail, lax.rem(z, 4)], sem_a.at[z], dev(z_=to))
+    arrived(XI.at[z], sem_i.at[z])
+    pltpu.make_async_copy(XI.at[z], X.at[c, upper, lead, trail, lax.rem(z, 4)], sem_a.at[z]).start()
 
     lane8 = lax.broadcasted_iota(jnp.int32, (8, 128), 1)
     starts = jnp.full((8, 128), 1 << 20, jnp.int32)
@@ -112,115 +162,146 @@
     start_of = jnp.max(jnp.where(starts <= t_wide, starts, 0.0), axis=1, keepdims=True)
     t_col = t_wide[:, 0:1]
     into = t_col - start_of
-    row8 = lane8
     bias_row = jnp.zeros((8, 128), F32)
     rate_row = jnp.zeros((8, 128), F32)
     lane_256 = lax.broadcasted_iota(jnp.int32, (8, 256), 1)
     skip_row = jnp.zeros((8, 256), F32)
     for i in range(4):
-        bias_row = jnp.where(row8 == STEP0 + i, bias[4 * c + i], bias_row)
-        rate_row = jnp.where(row8 == STEP0 + i, rate[4 * c + i], rate_row)
+        bias_row = jnp.where(lane8 == STEP0 + i, bias[4 * c + i], bias_row)
+        rate_row = jnp.where(lane8 == STEP0 + i, rate[4 * c + i], rate_row)
         skip_row = jnp.where(lax.div(lane_256, 64) == i, skip[4 * c + i], skip_row)
     bias_row, rate_row, skip_row = bias_row[0:1], rate_row[0:1], skip_row[0:1]
 
-    for zt in range(8):
-        arrived(X.at[c, x, y, zt], sem_a.at[zt])
-    mine = X.at[c, x, y]
-    send(mine, mine, sem_y.at[y], dev(y_=m4(y + 1)))
-    send(mine, mine, sem_y.at[y], dev(y_=m4(y - 1)))
-    near = X.at[c, x, m4(y - sg)]
-    arrived(near, sem_y.at[m4(y - sg)])
-    send(near, near, sem_y.at[m4(y - sg)], dev(y_=m4(y + sg)))
-    arrived(X.at[c, x, m4(y + sg)], sem_y.at[m4(y + sg)])
-    arrived(X.at[c, x, m4(y + 2)], sem_y.at[m4(y + 2)])
-    mine = X.at[c, x]
-    send(mine, mine, sem_s.at[x], sibling)
-    send(mine, mine, sem_x.at[x], dev(x_=m4(x + 1)))
-    send(mine, mine, sem_x.at[x], dev(x_=m4(x - 1)))
-    arrived(W.at[1 - c], sem_w)
+    def at_x(q):
+        return dev(x_=q)
+
+    def at_y(q):
+        return dev(y_=q)
+
+    legs = [(x, at_x, y, at_y), (y, at_y, x, at_x)]
+    for h, (a, _, b, to) in enumerate(legs):
+        for zt in range(4):
+            arrived(X.at[c, h, a, b, zt], sem_a.at[4 * h + zt])
+        mine = X.at[c, h, a, b]
+        send(mine, mine, sem_y.at[h, b], to(m4(b + 1)))
+        send(mine, mine, sem_y.at[h, b], to(m4(b - 1)))
+    for h, (a, _, b, to) in enumerate(legs):
+        near = X.at[c, h, a, m4(b - sg)]
+        arrived(near, sem_y.at[h, m4(b - sg)])
+        send(near, near, sem_y.at[h, m4(b - sg)], to(m4(b + sg)))
+    for h, (a, to, b, _) in enumerate(legs):
+        for q in (m4(b + sg), m4(b + 2)):
+            arrived(X.at[c, h, a, q], sem_y.at[h, q])
+        mine = X.at[c, h, a]
+        send(mine, mine, sem_s.at[h, a], sibling)
+        send(mine, mine, sem_x.at[h, a], to(m4(a + 1)))
+        send(mine, mine, sem_x.at[h, a], to(m4(a - 1)))
+    arrived(WV.at[1 - c], sem_w.at[0])
+    arrived(WG.at[1 - c], sem_w.at[1])
 
     lane_e = lax.broadcasted_iota(jnp.int32, (256, 128), 1)
-
-    def product(g, xg):
-        other = X.at[1 - c, xg]
-        arrived(other, sem_s.at[xg])
-
-        def half(i, carry):
-            a = X[0, xg, pl.ds(2 * i, 2)].reshape(256, 512)
-            b = X[1, xg, pl.ds(2 * i, 2)].reshape(256, 512)
-            p = dot(a, W[0]) + dot(b, W[1])
+    groups = [[a, m4(a - sg), m4(a + sg), m4(a + 2)] for a, _, _, _ in legs]
+
+    def came(j):
+        for h, (a, to, _, _) in enumerate(legs):
+            q = groups[h][j]
+            got = X.at[c, h, q]
+            arrived(got, sem_x.at[h, q])
+            if j == 1:
+                send(got, got, sem_x.at[h, q], to(m4(a + sg)))
+            send(got, got, sem_s.at[h, q], sibling)
+
+    def product(g):
+        for h in range(2):
+            arrived(X.at[1 - c, h, groups[h][g]], sem_s.at[h, groups[h][g]])
+            a = X[0, h, groups[h][g]].reshape(256, 512)
+            b = X[1, h, groups[h][g]].reshape(256, 512)
+            p = dot(a, WV[0]) + dot(b, WV[1])
+            PG[g, h] = (dot(a, WG[0]) + dot(b, WG[1])).reshape(4, 4, 16, 256)
             a, b = a.astype(F32), b.astype(F32)
             squares = jnp.sum(a * a + b * b, axis=1, keepdims=True)
-            PS[g, pl.ds(2 * i, 2), :, :, 0:512] = p[:, 0:512].reshape(2, 8, 16, 512)
-            PS[g, pl.ds(2 * i, 2), :, :, 512:640] = (
-                p[:, 512:640] + jnp.where(lane_e == SQ, squares, 0.0)
-            ).reshape(2, 8, 16, 128)
-            return carry
-
-        lax.fori_loop(0, 2, half, 0)
-
-    def hop(g, k):
+            PV[g, h, :, :, :, 0:256] = p[:, 0:256].reshape(4, 4, 16, 256)
+            PV[g, h, :, :, :, 256:384] = (p[:, 256:384] + jnp.where(lane_e == SQ, squares, 0.0)).reshape(4, 4, 16, 128)
+
+    rings = [
+        (0, 1, "all", S0L, S0S, R0L, R0S),
+        (1, 2, "values", S1L, S1S, R1L, R1S),
+        (3, 1, "values", S2L, S2S, R2L, R2S),
+        (1, 3, "gate", S3L, S3S, R3L, R3S),
+    ]
+
+    def pieces(r, d):
+        g, n, kind = rings[r][:3]
+        d_up, d_at = lax.div(d, 4), lax.rem(d, 4)
+        got = []
+        if kind != "gate":
+            got.append((0, 384, PV[pl.ds(g, n), d_up, :, d_at]))
+        if kind != "values":
+            got.append((got[0][1] if got else 0, 256, PG[pl.ds(g, n), d_up, :, d_at]))
+        return got
+
+    def hop(r, k):
+        out_l, out_s, in_l, in_s = rings[r][3:]
         if k:
-            arrived(RL.at[g, k - 1], sem_l.at[g, k - 1])
-        long = PS[g, :, m8(z + (4 - k) * sg)]
-        SL[g, k] = (long + RL[g, k - 1].astype(F32) if k else long).astype(BF16)
-        send(SL.at[g, k], RL.at[g, k], sem_l.at[g, k], dev(z_=m8(z + sg)))
+            arrived(in_l.at[k - 1], sem_l.at[r, k - 1])
+        for lo, wide, v in pieces(r, m8(z + (4 - k) * sg)):
+            if k:
+                v = v + in_l[k - 1, :, :, :, lo : lo + wide].astype(F32)
+            out_l[k, :, :, :, lo : lo + wide] = v.astype(BF16)
+        send(out_l.at[k], in_l.at[k], sem_l.at[r, k], dev(z_=m8(z + sg)))
         if k < 3:
             if k:
-                arrived(RS.at[g, k - 1], sem_sh.at[g, k - 1])
-            short = PS[g, :, m8(z - (3 - k) * sg)]
-            SS[g, k] = (short + RS[g, k - 1].astype(F32) if k else short).astype(BF16)
-            send(SS.at[g, k], RS.at[g, k], sem_sh.at[g, k], dev(z_=m8(z - sg)))
-
-    def last(g, xg):
-        arrived(RL.at[g, 3], sem_l.at[g, 3])
-        arrived(RS.at[g, 2], sem_sh.at[g, 2])
-        R[xg] = PS[g, :, z] + RL[g, 3].astype(F32) + RS[g, 2].astype(F32)
-
-    groups = [x, m4(x - sg), m4(x + sg), m4(x + 2)]
-
-    def came(j):
-        got = X.at[c, groups[j]]
-        arrived(got, sem_x.at[groups[j]])
-        if j == 1:
-            send(got, got, sem_x.at[groups[j]], dev(x_=m4(x + sg)))
-        send(got, got, sem_s.at[groups[j]], sibling)
-
-    product(0, groups[0])
-    for k in range(4):
-        hop(0, k)
+                arrived(in_s.at[k - 1], sem_sh.at[r, k - 1])
+            for lo, wide, v in pieces(r, m8(z - (3 - k) * sg)):
+                if k:
+                    v = v + in_s[k - 1, :, :, :, lo : lo + wide].astype(F32)
+                out_s[k, :, :, :, lo : lo + wide] = v.astype(BF16)
+            send(out_s.at[k], in_s.at[k], sem_sh.at[r, k], dev(z_=m8(z - sg)))
+
+    def last(r):
+        g, n, kind, _, _, in_l, in_s = rings[r]
+        arrived(in_l.at[3], sem_l.at[r, 3])
+        arrived(in_s.at[2], sem_sh.at[r, 2])
+        for lo, wide, v in pieces(r, z):
+            v = v + in_l[3, :, :, :, lo : lo + wide].astype(F32) + in_s[2, :, :, :, lo : lo + wide].astype(F32)
+            ref = RV if wide == 384 else RG
+            for j in range(n):
+                a = groups[0][g + j] + upper * (groups[1][g + j] - groups[0][g + j])
+                for i in range(4):
+                    ref[a + upper * (i - a), i + upper * (a - i)] = v[j, i]
+
+    product(0)
+    hop(0, 0)
+    hop(0, 1)
+    hop(0, 2)
     came(1)
     came(2)
-    product(1, groups[1])
+    product(1)
+    product(2)
     hop(1, 0)
-    last(0, groups[0])
-    product(2, groups[2])
+    hop(0, 3)
+    hop(1, 1)
+    came(3)
+    product(3)
     hop(2, 0)
-    hop(1, 1)
+    hop(1, 2)
+    last(0)
     hop(2, 1)
-    hop(1, 2)
+    hop(1, 3)
+    hop(3, 0)
     hop(2, 2)
-    hop(1, 3)
-    came(3)
-    product(3, groups[3])
-    hop(3, 0)
+    last(1)
     hop(2, 3)
-    last(1, groups[1])
     hop(3, 1)
-    last(2, groups[2])
-    hop(3, 2)
-    hop(3, 3)
-    last(3, groups[3])
-
-    scale = lax.rsqrt(R[:, :, :, 512:640].reshape(256, 128)[:, SQ : SQ + 1] * (1.0 / 8192) + EPSILON)
-    raw = (R[:, :, :, 256:640].reshape(256, 384) * scale).astype(BF16)
+    last(2)
+
+    scale = lax.rsqrt(RV[:, :, :, 256:384].reshape(256, 128)[:, SQ : SQ + 1] * (1.0 / 8192) + EPSILON)
+    raw = (RV[...].reshape(256, 384) * scale).astype(BF16)
     HS[...] = raw[240:256]
     send(HS, HR, sem_h, dev(z_=m8(z + 1)))
     EXT[16:272] = raw.astype(F32)
-    gate = R[:, :, :, 0:256].reshape(256, 256) * scale
-    GS[...] = gate * jax.nn.sigmoid(gate)
-
-    raw_step = R[:, :, :, 512:640].reshape(256, 128) * scale + bias_row
+
+    raw_step = RV[:, :, :, 256:384].reshape(256, 128) * scale + bias_row
     step = jnp.maximum(raw_step, 0.0) + jnp.log1p(jnp.exp(-jnp.abs(raw_step)))
     log_decay = -rate_row * step
     order_r = lax.broadcasted_iota(jnp.int32, (256, 256), 0)
@@ -255,7 +336,6 @@
             acc = acc + jnp.where(into >= 3 - k, EXT[13 + k : 269 + k, lo : lo + width], 0.0) * taps[k]
         return acc * jax.nn.sigmoid(acc)
 
-    turn = lax.rem(128 - 32 * y, 128)
     maps_cols = pl.ds(pl.multiple_of(128 * c, 128), 128)
     group_row = lax.broadcasted_iota(jnp.int32, (4, 128), 0) == x
     taps_s = [
@@ -270,11 +350,11 @@
     ]
     maps = jnp.transpose(conv(256, 128, taps_s))[0:32].astype(BF16)
     BC[c, y] = maps
-    peers = [(dc, dy) for dc in range(2) for dy in range(4) if (dc, dy) != (0, 0)]
     for dc, dy in peers:
         to_c = lax.rem(c + dc, 2)
         send(BC.at[c, y], BC.at[c, y], sem_bc.at[4 * c + y], dev(c_=to_c, y_=m4(y + dy)))
 
+    hop(3, 2)
     own_cols = pl.ds(pl.multiple_of(256 * c, 256), 256)
     inputs = conv(0, 256, [conv_v[k : k + 1, own_cols] for k in range(4)]).astype(BF16).astype(F32)
     stepped = inputs * step_wide
@@ -295,6 +375,7 @@
         send(ST.at[k], SR.at[z], sem_st.at[z], dev(z_=k))
     SR[z] = ST[z]
 
+    hop(3, 3)
     scores = dot(c_cols, b_rows)
     parts = []
     for i in range(4):
@@ -319,7 +400,19 @@
         k = m8(z + o)
         arrived(SI.at[k], sem_in.at[k])
     outputs = partly + dot(c_cols, SI[...].reshape(128, 256)) * carried
-    gated = outputs * GS[...]
+    last(3)
+    gate = RG[...].reshape(256, 256) * scale
+    gated = outputs * (gate * jax.nn.sigmoid(gate))
+    GZ[c, z] = (gated * mix_gain[0:1, own_cols]).astype(BF16)
+
+    order = [z]
+    for k in range(1, 4):
+        order += [m8(z - k * sg), m8(z + k * sg)]
+    order.append(m8(z + 4))
+    block = GZ.at[c, z]
+    send(block, block, sem_g.at[z], dev(z_=m8(z + sg)))
+    send(block, block, sem_g.at[z], dev(z_=m8(z - sg)))
+    send(block, block, sem_gs.at[z], sibling)
 
     own_sq = 2 * y + c
     SQB[own_sq] = lax.dot_general(
@@ -330,19 +423,9 @@
     for dc, dy in peers:
         k = 2 * m4(y + dy) + lax.rem(c + dc, 2)
         arrived(SQB.at[k], sem_sq.at[k])
-    squares = jnp.sum(SQB[...], axis=0)
-    norm = lax.rsqrt(squares * (1.0 / 2048) + EPSILON)
-    norm = jnp.transpose(jnp.concatenate([norm] * 16, axis=0))[:, 0:1]
-    GZ[c, z] = (gated * norm * mix_gain[0:1, own_cols]).astype(BF16)
-
-    order = [z]
-    for k in range(1, 4):
-        order += [m8(z - k * sg), m8(z + k * sg)]
-    order.append(m8(z + 4))
-    block = GZ.at[c, z]
-    send(block, block, sem_g.at[z], dev(z_=m8(z + sg)))
-    send(block, block, sem_g.at[z], dev(z_=m8(z - sg)))
-    send(block, block, sem_gs.at[z], sibling)
+    NZ[z] = lax.rsqrt(jnp.sum(SQB[...], axis=0) * (1.0 / 2048) + EPSILON)
+    for o in range(1, 8):
+        send(NZ.at[z], NZ.at[z], sem_nz.at[z], dev(z_=m8(z + o)))
 
     def pass_on(o):
         zt = order[o]
@@ -361,7 +444,10 @@
             if o < 7:
                 pass_on(o + 1)
         arrived(GZ.at[1 - c, zt], sem_gs.at[zt])
-        T[o] = (dot(GZ[0, zt], out_w[0:256]) + dot(GZ[1, zt], out_w[256:512])).reshape(4, 4, 16, 512)
+        if o:
+            arrived(NZ.at[zt], sem_nz.at[zt])
+        norm = jnp.transpose(jnp.concatenate([NZ[zt]] * 16, axis=0))[:, 0:1]
+        T[o] = ((dot(GZ[0, zt], out_w[0:256]) + dot(GZ[1, zt], out_w[256:512])) * norm).reshape(4, 4, 16, 512)
 
     def along(o, level):
         over_x = (o % 2 == 0) == (level == 1)
@@ -438,32 +524,14 @@
         arrived(FR.at[i], sem_f.at[i])
     out[...] = (tok[...].astype(F32) + FR[...].reshape(128, 512).astype(F32)).astype(BF16)
 
-    for copy, away in started:
-        if away is None:
-            copy.wait_send()
-        else:
-
-            @pl.when(away)
-            def _(copy=copy):
-                copy.wait_send()
-
-    assert len(started) <= SENDS
+    wrap_up()
 
 
 def local(
     tokens, norm_gain, gate_proj, value_proj, step_proj, state_proj, conv_value, conv_state, step_bias, decay_rate,
     skip_gain, mix_gain, out_proj, doc_lengths,
 ):
-    f = lax.axis_index("fsdp")
-    x, y = f // 4, f % 4
-    rows = state_proj.shape[0]
-    halves = []
-    for core in range(2):
-        maps = lax.dynamic_slice(state_proj, (0, x, 128 * core + 32 * y), (rows, 1, 32))[:, 0]
-        halves.append(
-            jnp.concatenate([maps, step_proj[:, 4 * core : 4 * core + 4], jnp.zeros((rows, 92), BF16)], axis=1)
-        )
-    extra = jnp.stack(halves)
+    maps = lax.dynamic_index_in_dim(state_proj, lax.axis_index("fsdp") // 4, 1, keepdims=False)
     vmem = pl.BlockSpec(memory_space=pltpu.VMEM)
     smem = pl.BlockSpec(memory_space=pltpu.SMEM)
 
@@ -476,18 +544,22 @@
     return pl.pallas_call(
         body,
         out_shape=jax.ShapeDtypeStruct((128, 512), BF16),
-        in_specs=[vmem] * 9 + [smem] * 4,
+        in_specs=[vmem] * 10 + [smem] * 4,
         out_specs=vmem,
         scratch_shapes=[
-            buf(2, 4, 4, 8, 16, 512),
-            buf(2, 512, WIDE),
-            buf(512, WIDE),
-            buf(4, 4, 8, 16, WIDE, dtype=F32),
-            buf(4, 4, 4, 16, WIDE),
-            buf(4, 3, 4, 16, WIDE),
-            buf(4, 4, 4, 16, WIDE),
-            buf(4, 3, 4, 16, WIDE),
-            buf(4, 4, 16, WIDE, dtype=F32),
+            buf(8, 16, 512),
+            buf(2, 2, 4, 4, 4, 16, 512),
+            buf(2, 512, 384),
+            buf(2, 512, 256),
+            buf(512, 384),
+            buf(512, 256),
+            buf(4, 2, 4, 4, 16, 384, dtype=F32),
+            buf(4, 2, 4, 4, 16, 256, dtype=F32),
+        ]
+        + [buf(k, n, 4, 16, w) for n, w in ((1, 640), (2, 384), (1, 384), (3, 256)) for k in (4, 3, 4, 3)]
+        + [
+            buf(4, 4, 16, 384, dtype=F32),
+            buf(4, 4, 16, 256, dtype=F32),
             buf(16, 384),
             buf(16, 384),
             buf(272, 384, dtype=F32),
@@ -496,7 +568,7 @@
             buf(8, 32, 256),
             buf(8, 16, 256),
             buf(8, 16, 256),
-            buf(256, 256, dtype=F32),
+            buf(8, 8, 256, dtype=F32),
             buf(8, 8, 256, dtype=F32),
             buf(2, 8, 256, 256),
             buf(8, 4, 4, 16, 512, dtype=F32),
@@ -506,13 +578,13 @@
         + [buf(8, 16, 512)] * 6
         + [buf(8, 16, 512)] * 2
         + [
-            dma(SENDS), dma(8), dma(4), dma(4), dma(4), dma(), dma(4, 4), dma(4, 3), dma(), dma(8), dma(8), dma(8),
-            dma(8), dma(8), dma(8), dma(8, 3), dma(8, 3), dma(8), dma(),
+            dma(SENDS), dma(8), dma(8), dma(2, 4), dma(2, 4), dma(2, 4), dma(2), dma(4, 4), dma(4, 3), dma(), dma(8),
+            dma(8), dma(8), dma(8), dma(8), dma(8), dma(8), dma(8, 3), dma(8, 3), dma(8),
         ],
-        compiler_params=pltpu.CompilerParams(has_side_effects=True, vmem_limit_bytes=56 * 2**20),
+        compiler_params=pltpu.CompilerParams(collective_id=0, has_side_effects=True, vmem_limit_bytes=56 * 2**20),
         name="mixer",
     )(
-        tokens, norm_gain.reshape(1, -1), gate_proj, value_proj, extra, conv_value, conv_state, mix_gain.reshape(1, -1),
+        tokens, norm_gain.reshape(1, -1), gate_proj, value_proj, maps, step_proj.T, conv_value, conv_state, mix_gain.reshape(1, -1),
         out_proj, step_bias, decay_rate, skip_gain, doc_lengths,
     )
 

time: 164 us -> 138 us (0.84)
  Pallas kernels: 158 us -> 134 us
    pallas_call x1, Pallas kernels: 158 us -> 134 us  [local(): pl.pallas_call(body, out_shape=jax.ShapeDtypeStruct((128, 512), BF16), in...]
    unnamed x3 -> x4, local copies, waits for them, and re-layouts: 2.22 us -> 3.53 us
where the time goes in v2:
time: 138 us
  Pallas kernels  134 us (97%)
  local copies, waits for them, and re-layouts  4.07 us (3%)
    pallas_call x1, Pallas kernels, local(): pl.pallas_call(body, out_shape=jax.ShapeDtypeStruct((128, 512), BF16), in...  134 us
    unnamed x4, local copies, waits for them, and re-layouts  3.53 us

profile of v2, /device:TPU:4, one launch (start us, length us, event | category | flops | bytes accessed | tf_op | source)
XLA Modules:
  0.0 137.9 jit_solution(8879960927297853657)
XLA Ops:
  0.0 0.0 copy-start
  0.0 1.2 copy-done
  1.2 0.5 constant_dynamic-slice_fusion
  1.8 0.7 copy.18
  2.5 133.8 %mixer.1 = bf16[128,512]{1,0:T(8,128)(2,1)} custom-call(bf16[128,512]{1,0:T(8,128)(2,1)} %tok.1, f32[1,8192]{1,0:T(1,128)} %bitcast.7, bf16[512,512]{1,0:T(8,128)(2,1)} %gate_w.1, bf16[512,512]{1,0:T(8,128)(2,1)} %value_w.1, bf16[512,256]{1,0:T(8,128)(2,1)} %bitcast.6, bf16[8,512]{1,0:T(8,128)(2,1)} %bitcast.8, f32[4,512]{1,0:T(4,128)} %conv_v.1, ...), custom_call_target="tpu_custom_call" | custom-call | tf_op jit(solution)/shard_map/mixer/pallas_call | solution.py:544
  136.3 1.6 %copy.20 = bf16[128,512]{1,0:T(8,128)(2,1)} copy(bf16[128,512]{1,0:T(8,128)(2,1)} %mixer.1) | data formatting | bytes 262144
Async XLA Ops:
  0.0 1.2 copy-start

commit v3 on v2

--- a/solution.py
+++ b/solution.py
@@ -14,7 +14,7 @@
 WIDE = 640
 STEP0 = 32
 SQ = 40
-SENDS = 260
+SENDS = 320
 
 
 def dot(a, b, precision=None):
@@ -22,14 +22,15 @@
 
 
 def body(
-    tok, gain, gate_w, value_w, maps_w, step_w, conv_v, conv_s, mix_gain, out_w,
+    tok_h, gain_h, gate_h, value_h, maps_h, step_h, conv_v_h, conv_s_h, mix_gain_h, out_w_h,
     bias, rate, skip, docs,
     out,
+    tok, gain, gate_w, value_w, maps_w, step_w, conv_v, conv_s, mix_gain, out_w,
     XI, X, WV, WG, SV, SG, PV, PG, S0L, S0S, R0L, R0S, S1L, S1S, R1L, R1S, S2L, S2S, R2L, R2S, S3L, S3S, R3L, R3S, RV, RG,
     HS, HR, EXT, BC, ST, SR, SO, SI, SQB, NZ, GZ, T, Q, A1, B1, C1, RA1, RB1, RC1,
     A2, B2, C2, RA2, RB2, RC2, FO, FR,
-    sem_send, sem_i, sem_a, sem_y, sem_x, sem_s, sem_w, sem_l, sem_sh, sem_h, sem_bc, sem_st, sem_in, sem_sq, sem_nz,
-    sem_g, sem_gs, sem_1, sem_2, sem_f,
+    sem_load, sem_send, sem_i, sem_a, sem_y, sem_x, sem_s, sem_w, sem_l, sem_sh, sem_h, sem_bc, sem_st, sem_in, sem_sq,
+    sem_nz, sem_g, sem_gs, sem_1, sem_2, sem_f,
 ):
     s = lax.axis_index("seq")
     f = lax.axis_index("fsdp")
@@ -112,6 +113,19 @@
         greet(dev(c_=lax.rem(c + dc, 2), y_=m4(y + dy)))
     greet(dev(x_=m4(x + 1)))
     greet(dev(x_=m4(x - 1)))
+
+    loads = [
+        pltpu.make_async_copy(src, dst, sem_load.at[i])
+        for i, (src, dst) in enumerate(
+            (
+                (tok_h, tok), (gain_h, gain), (value_h, value_w), (maps_h, maps_w), (step_h, step_w), (gate_h, gate_w),
+                (conv_v_h, conv_v), (conv_s_h, conv_s), (mix_gain_h, mix_gain), (out_w_h, out_w),
+            )
+        )
+    ]
+    for load in loads:
+        load.start()
+    loads[1].wait()
 
     gain_col = jnp.transpose(
         jnp.broadcast_to(gain[0:1, pl.ds(pl.multiple_of(512 * s, 512), 512)], (128, 512))
@@ -129,6 +143,8 @@
         ref_v[:, 256:384] = (extra * gain_col).astype(BF16)
         ref_g[...] = (gate_w[:, cols].astype(F32) * gain_col).astype(BF16)
 
+    for load in (loads[0], *loads[2:]):
+        load.wait()
     pl.semaphore_wait(barrier, 32 - 2 * own_leg.astype(jnp.int32))
 
     for i in range(8):
@@ -179,23 +195,42 @@
         return dev(y_=q)
 
     legs = [(x, at_x, y, at_y), (y, at_y, x, at_x)]
+    def spread(h, q):
+        a, to, _, _ = legs[h]
+        mine = X.at[c, h, a, q]
+        send(mine, mine, sem_x.at[h, a, q], to(m4(a + 1)))
+        send(mine, mine, sem_x.at[h, a, q], to(m4(a - 1)))
+
+    def relay(h, q):
+        a, to, _, _ = legs[h]
+        near = m4(a - sg)
+        got = X.at[c, h, near, q]
+        arrived(got, sem_x.at[h, near, q])
+        send(got, got, sem_x.at[h, near, q], to(m4(a + sg)))
+
+    def trailing(h, q):
+        arrived(X.at[c, h, legs[h][0], q], sem_y.at[h, q])
+
     for h, (a, _, b, to) in enumerate(legs):
         for zt in range(4):
             arrived(X.at[c, h, a, b, zt], sem_a.at[4 * h + zt])
         mine = X.at[c, h, a, b]
         send(mine, mine, sem_y.at[h, b], to(m4(b + 1)))
         send(mine, mine, sem_y.at[h, b], to(m4(b - 1)))
+        spread(h, b)
     for h, (a, _, b, to) in enumerate(legs):
         near = X.at[c, h, a, m4(b - sg)]
-        arrived(near, sem_y.at[h, m4(b - sg)])
+        trailing(h, m4(b - sg))
         send(near, near, sem_y.at[h, m4(b - sg)], to(m4(b + sg)))
-    for h, (a, to, b, _) in enumerate(legs):
-        for q in (m4(b + sg), m4(b + 2)):
-            arrived(X.at[c, h, a, q], sem_y.at[h, q])
-        mine = X.at[c, h, a]
-        send(mine, mine, sem_s.at[h, a], sibling)
-        send(mine, mine, sem_x.at[h, a], to(m4(a + 1)))
-        send(mine, mine, sem_x.at[h, a], to(m4(a - 1)))
+        spread(h, m4(b - sg))
+        trailing(h, m4(b + sg))
+        spread(h, m4(b + sg))
+    for h, (_, _, b, _) in enumerate(legs):
+        relay(h, b)
+    for h, (a, _, b, _) in enumerate(legs):
+        trailing(h, m4(b + 2))
+        spread(h, m4(b + 2))
+        send(X.at[c, h, a], X.at[c, h, a], sem_s.at[h, a], sibling)
     arrived(WV.at[1 - c], sem_w.at[0])
     arrived(WG.at[1 - c], sem_w.at[1])
 
@@ -203,13 +238,12 @@
     groups = [[a, m4(a - sg), m4(a + sg), m4(a + 2)] for a, _, _, _ in legs]
 
     def came(j):
-        for h, (a, to, _, _) in enumerate(legs):
+        for h, (_, _, b, _) in enumerate(legs):
             q = groups[h][j]
-            got = X.at[c, h, q]
-            arrived(got, sem_x.at[h, q])
-            if j == 1:
-                send(got, got, sem_x.at[h, q], to(m4(a + sg)))
-            send(got, got, sem_s.at[h, q], sibling)
+            for at in range(4):
+                if j > 1:
+                    arrived(X.at[c, h, q, at], sem_x.at[h, q, at])
+            send(X.at[c, h, q], X.at[c, h, q], sem_s.at[h, q], sibling)
 
     def product(g):
         for h in range(2):
@@ -272,27 +306,31 @@
 
     product(0)
     hop(0, 0)
+    for at in (-1, 1):
+        for h in range(2):
+            relay(h, m4(legs[h][2] + at * sg))
     hop(0, 1)
-    hop(0, 2)
+    for h in range(2):
+        relay(h, m4(legs[h][2] + 2))
     came(1)
     came(2)
     product(1)
     product(2)
     hop(1, 0)
-    hop(0, 3)
-    hop(1, 1)
+    hop(0, 2)
     came(3)
     product(3)
     hop(2, 0)
+    hop(1, 1)
+    hop(0, 3)
+    hop(2, 1)
     hop(1, 2)
     last(0)
-    hop(2, 1)
+    hop(2, 2)
     hop(1, 3)
+    hop(2, 3)
     hop(3, 0)
-    hop(2, 2)
     last(1)
-    hop(2, 3)
-    hop(3, 1)
     last(2)
 
     scale = lax.rsqrt(RV[:, :, :, 256:384].reshape(256, 128)[:, SQ : SQ + 1] * (1.0 / 8192) + EPSILON)
@@ -329,6 +367,7 @@
 
     arrived(HR, sem_h)
     EXT[0:16] = HR[...].astype(F32)
+    hop(3, 1)
 
     def conv(lo, width, taps):
         acc = jnp.zeros((256, width), F32)
@@ -354,7 +393,6 @@
         to_c = lax.rem(c + dc, 2)
         send(BC.at[c, y], BC.at[c, y], sem_bc.at[4 * c + y], dev(c_=to_c, y_=m4(y + dy)))
 
-    hop(3, 2)
     own_cols = pl.ds(pl.multiple_of(256 * c, 256), 256)
     inputs = conv(0, 256, [conv_v[k : k + 1, own_cols] for k in range(4)]).astype(BF16).astype(F32)
     stepped = inputs * step_wide
@@ -364,6 +402,7 @@
     for dc, dy in peers:
         pc, py = lax.rem(c + dc, 2), m4(y + dy)
         arrived(BC.at[pc, py], sem_bc.at[4 * pc + py])
+    hop(3, 2)
     b_rows = BC[0].reshape(128, 256)
     c_cols = jnp.transpose(BC[1].reshape(128, 256).astype(F32)).astype(BF16)
 
@@ -375,7 +414,6 @@
         send(ST.at[k], SR.at[z], sem_st.at[z], dev(z_=k))
     SR[z] = ST[z]
 
-    hop(3, 3)
     scores = dot(c_cols, b_rows)
     parts = []
     for i in range(4):
@@ -396,6 +434,7 @@
         k = m8(z + o)
         send(SO.at[k], SI.at[z], sem_in.at[z], dev(z_=k))
     SI[z] = SO[z]
+    hop(3, 3)
     for o in range(1, 8):
         k = m8(z + o)
         arrived(SI.at[k], sem_in.at[k])
@@ -403,16 +442,17 @@
     last(3)
     gate = RG[...].reshape(256, 256) * scale
     gated = outputs * (gate * jax.nn.sigmoid(gate))
-    GZ[c, z] = (gated * mix_gain[0:1, own_cols]).astype(BF16)
+    GZ[c, z] = (gated * mix_gain[0:1, own_cols]).astype(BF16).reshape(2, 128, 256)
 
     order = [z]
     for k in range(1, 4):
         order += [m8(z - k * sg), m8(z + k * sg)]
     order.append(m8(z + 4))
-    block = GZ.at[c, z]
-    send(block, block, sem_g.at[z], dev(z_=m8(z + sg)))
-    send(block, block, sem_g.at[z], dev(z_=m8(z - sg)))
-    send(block, block, sem_gs.at[z], sibling)
+    for i in range(2):
+        block = GZ.at[c, z, i]
+        send(block, block, sem_g.at[z, i], dev(z_=m8(z + sg)))
+        send(block, block, sem_g.at[z, i], dev(z_=m8(z - sg)))
+        send(block, block, sem_gs.at[z, i], sibling)
 
     own_sq = 2 * y + c
     SQB[own_sq] = lax.dot_general(
@@ -427,27 +467,29 @@
     for o in range(1, 8):
         send(NZ.at[z], NZ.at[z], sem_nz.at[z], dev(z_=m8(z + o)))
 
-    def pass_on(o):
+    def pass_on(o, i):
         zt = order[o]
-        got = GZ.at[c, zt]
-        arrived(got, sem_g.at[zt])
+        got = GZ.at[c, zt, i]
+        arrived(got, sem_g.at[zt, i])
         if o in (1, 3, 5):
-            send(got, got, sem_g.at[zt], dev(z_=m8(z + sg)))
+            send(got, got, sem_g.at[zt, i], dev(z_=m8(z + sg)))
         if o in (2, 4):
-            send(got, got, sem_g.at[zt], dev(z_=m8(z - sg)))
-        send(got, got, sem_gs.at[zt], sibling)
+            send(got, got, sem_g.at[zt, i], dev(z_=m8(z - sg)))
+        send(got, got, sem_gs.at[zt, i], sibling)
 
     def take(o):
         zt = order[o]
         if o % 2 == 1:
-            pass_on(o)
-            if o < 7:
-                pass_on(o + 1)
-        arrived(GZ.at[1 - c, zt], sem_gs.at[zt])
+            for i in range(2):
+                pass_on(o, i)
+                if o < 7:
+                    pass_on(o + 1, i)
+        for i in range(2):
+            arrived(GZ.at[1 - c, zt, i], sem_gs.at[zt, i])
         if o:
             arrived(NZ.at[zt], sem_nz.at[zt])
         norm = jnp.transpose(jnp.concatenate([NZ[zt]] * 16, axis=0))[:, 0:1]
-        T[o] = ((dot(GZ[0, zt], out_w[0:256]) + dot(GZ[1, zt], out_w[256:512])) * norm).reshape(4, 4, 16, 512)
+        T[o] = ((dot(GZ[0, zt].reshape(256, 256), out_w[0:256]) + dot(GZ[1, zt].reshape(256, 256), out_w[256:512])) * norm).reshape(4, 4, 16, 512)
 
     def along(o, level):
         over_x = (o % 2 == 0) == (level == 1)
@@ -461,12 +503,17 @@
     def quarter(o, q):
         return T[o, q] if o % 2 == 0 else T[o, :, q]
 
+    straight = (6, 7)
+
     def first_out(o):
         p, to = along(o, 1)
         A1[o] = quarter(o, m4(p + 2)).astype(BF16)
-        send(A1.at[o], RA1.at[o], sem_1.at[o, 0], to(m4(p + sg)))
+        send(A1.at[o], RA1.at[o], sem_1.at[o, 0], to(m4(p + 2) if o in straight else m4(p + sg)))
         B1[o] = quarter(o, m4(p - sg)).astype(BF16)
         send(B1.at[o], RB1.at[o], sem_1.at[o, 1], to(m4(p - sg)))
+        if o in straight:
+            C1[o] = quarter(o, m4(p + sg)).astype(BF16)
+            send(C1.at[o], RC1.at[o], sem_1.at[o, 2], to(m4(p + sg)))
 
     def first_relay(o):
         p, to = along(o, 1)
@@ -478,18 +525,15 @@
         p, _ = along(o, 1)
         arrived(RB1.at[o], sem_1.at[o, 1])
         arrived(RC1.at[o], sem_1.at[o, 2])
-        Q[o] = quarter(o, p) + RB1[o].astype(F32) + RC1[o].astype(F32)
+        summed = quarter(o, p) + RB1[o].astype(F32) + RC1[o].astype(F32)
+        if o in straight:
+            arrived(RA1.at[o], sem_1.at[o, 0])
+            summed = summed + RA1[o].astype(F32)
+        Q[o] = summed
         p, to = along(o, 2)
-        A2[o] = Q[o, m4(p + 2)].astype(BF16)
-        send(A2.at[o], RA2.at[o], sem_2.at[o, 0], to(m4(p + sg)))
-        B2[o] = Q[o, m4(p - sg)].astype(BF16)
-        send(B2.at[o], RB2.at[o], sem_2.at[o, 1], to(m4(p - sg)))
-
-    def second_relay(o):
-        p, to = along(o, 2)
-        arrived(RA2.at[o], sem_2.at[o, 0])
-        C2[o] = (Q[o, m4(p + sg)] + RA2[o].astype(F32)).astype(BF16)
-        send(C2.at[o], RC2.at[o], sem_2.at[o, 2], to(m4(p + sg)))
+        for i, (out_b, in_b, q) in enumerate(((A2, RA2, m4(p + 2)), (B2, RB2, m4(p - sg)), (C2, RC2, m4(p + sg)))):
+            out_b[o] = Q[o, q].astype(BF16)
+            send(out_b.at[o], in_b.at[o], sem_2.at[o, i], to(q))
 
     block_at = f
     row_block = lax.rem(block_at, 8)
@@ -497,9 +541,9 @@
 
     def finish(o):
         p, _ = along(o, 2)
-        arrived(RB2.at[o], sem_2.at[o, 1])
-        arrived(RC2.at[o], sem_2.at[o, 2])
-        FO[o] = (Q[o, p] + RB2[o].astype(F32) + RC2[o].astype(F32)).astype(BF16)
+        for i, in_b in enumerate((RA2, RB2, RC2)):
+            arrived(in_b.at[o], sem_2.at[o, i])
+        FO[o] = (Q[o, p] + RA2[o].astype(F32) + RB2[o].astype(F32) + RC2[o].astype(F32)).astype(BF16)
         to = (2 * order[o] + to_core, s)
         own = (to[0] == s) & (s == f) if o == 0 else None
         if own is None:
@@ -507,18 +551,19 @@
         else:
             send_or_keep(own, FO.at[o], FR.at[row_block], sem_f.at[row_block], to)
 
-    for tick in range(8 + 4):
+    for tick in range(8 + 2):
         if tick < 8:
             take(tick)
             first_out(tick)
-        if 0 <= tick - 1 < 8:
+        if 0 <= tick - 1 < 8 and tick - 1 not in straight:
             first_relay(tick - 1)
-        if 0 <= tick - 2 < 8:
+        if 2 <= tick < 9:
             second_out(tick - 2)
+        if tick == 8:
+            second_out(7)
         if 0 <= tick - 3 < 8:
-            second_relay(tick - 3)
-        if 0 <= tick - 4 < 8:
-            finish(tick - 4)
+            finish(tick - 3)
+    finish(7)
 
     for i in range(8):
         arrived(FR.at[i], sem_f.at[i])
@@ -544,9 +589,19 @@
     return pl.pallas_call(
         body,
         out_shape=jax.ShapeDtypeStruct((128, 512), BF16),
-        in_specs=[vmem] * 10 + [smem] * 4,
+        in_specs=[pl.BlockSpec(memory_space=pl.ANY)] * 10 + [smem] * 4,
         out_specs=vmem,
         scratch_shapes=[
+            buf(128, 512),
+            buf(1, 8192, dtype=F32),
+            buf(512, 512),
+            buf(512, 512),
+            buf(512, 256),
+            buf(8, 512),
+            buf(4, 512, dtype=F32),
+            buf(4, 4, 256, dtype=F32),
+            buf(1, 512, dtype=F32),
+            buf(512, 512),
             buf(8, 16, 512),
             buf(2, 2, 4, 4, 4, 16, 512),
             buf(2, 512, 384),
@@ -570,7 +625,7 @@
             buf(8, 16, 256),
             buf(8, 8, 256, dtype=F32),
             buf(8, 8, 256, dtype=F32),
-            buf(2, 8, 256, 256),
+            buf(2, 8, 2, 128, 256),
             buf(8, 4, 4, 16, 512, dtype=F32),
             buf(8, 4, 16, 512, dtype=F32),
         ]
@@ -578,8 +633,8 @@
         + [buf(8, 16, 512)] * 6
         + [buf(8, 16, 512)] * 2
         + [
-            dma(SENDS), dma(8), dma(8), dma(2, 4), dma(2, 4), dma(2, 4), dma(2), dma(4, 4), dma(4, 3), dma(), dma(8),
-            dma(8), dma(8), dma(8), dma(8), dma(8), dma(8), dma(8, 3), dma(8, 3), dma(8),
+            dma(10), dma(SENDS), dma(8), dma(8), dma(2, 4), dma(2, 4, 4), dma(2, 4), dma(2), dma(4, 4), dma(4, 3), dma(), dma(8),
+            dma(8), dma(8), dma(8), dma(8), dma(8, 2), dma(8, 2), dma(8, 3), dma(8, 3), dma(8),
         ],
         compiler_params=pltpu.CompilerParams(collective_id=0, has_side_effects=True, vmem_limit_bytes=56 * 2**20),
         name="mixer",

time: 138 us -> 131 us (0.949)
  Pallas kernels: 134 us -> 126 us
    pallas_call x1, Pallas kernels: 134 us -> 126 us  [local(): pl.pallas_call(body, out_shape=jax.ShapeDtypeStruct((128, 512), BF16), in...]
where the time goes in v3:
time: 131 us
  Pallas kernels  126 us (96%)
  local copies, waits for them, and re-layouts  4.07 us (3%)
    pallas_call x1, Pallas kernels, local(): pl.pallas_call(body, out_shape=jax.ShapeDtypeStruct((128, 512), BF16), in...  126 us
    unnamed x4, local copies, waits for them, and re-layouts  3.53 us

profile of v3, /device:TPU:4, one launch (start us, length us, event | category | flops | bytes accessed | tf_op | source)
XLA Modules:
  0.0 130.5 jit_solution(13571613201847250180)
XLA Ops:
  0.0 0.0 copy-start
  0.0 1.2 copy-done
  1.2 0.5 constant_dynamic-slice_fusion
  1.8 0.7 copy.18
  2.5 126.4 %mixer.1 = bf16[128,512]{1,0:T(8,128)(2,1)} custom-call(bf16[128,512]{1,0:T(8,128)(2,1)} %tok_h.1, f32[1,8192]{1,0:T(1,128)} %bitcast.7, bf16[512,512]{1,0:T(8,128)(2,1)} %gate_h.1, bf16[512,512]{1,0:T(8,128)(2,1)} %value_h.1, bf16[512,256]{1,0:T(8,128)(2,1)} %bitcast.6, bf16[8,512]{1,0:T(8,128)(2,1)} %bitcast.8, f32[4,512]{1,0:T(4,128)} %conv_v_h.1, ...), custom_call_target="tpu_custom_call" | custom-call | tf_op jit(solution)/shard_map/mixer/pallas_call | solution.py:589
  128.9 1.6 %copy.20 = bf16[128,512]{1,0:T(8,128)(2,1)} copy(bf16[128,512]{1,0:T(8,128)(2,1)} %mixer.1) | data formatting | bytes 262144
Async XLA Ops:
  0.0 1.2 copy-start

commit v4 on v3

--- a/solution.py
+++ b/solution.py
@@ -25,7 +25,7 @@
     tok_h, gain_h, gate_h, value_h, maps_h, step_h, conv_v_h, conv_s_h, mix_gain_h, out_w_h,
     bias, rate, skip, docs,
     out,
-    tok, gain, gate_w, value_w, maps_w, step_w, conv_v, conv_s, mix_gain, out_w,
+    tok, gain, gate_w, value_w, all_maps, step_w, conv_v, conv_s, mix_gain, out_w, maps_w,
     XI, X, WV, WG, SV, SG, PV, PG, S0L, S0S, R0L, R0S, S1L, S1S, R1L, R1S, S2L, S2S, R2L, R2S, S3L, S3S, R3L, R3S, RV, RG,
     HS, HR, EXT, BC, ST, SR, SO, SI, SQB, NZ, GZ, T, Q, A1, B1, C1, RA1, RB1, RC1,
     A2, B2, C2, RA2, RB2, RC2, FO, FR,
@@ -118,7 +118,7 @@
         pltpu.make_async_copy(src, dst, sem_load.at[i])
         for i, (src, dst) in enumerate(
             (
-                (tok_h, tok), (gain_h, gain), (value_h, value_w), (maps_h, maps_w), (step_h, step_w), (gate_h, gate_w),
+                (tok_h, tok), (gain_h, gain), (value_h, value_w), (maps_h, all_maps), (step_h, step_w), (gate_h, gate_w),
                 (conv_v_h, conv_v), (conv_s_h, conv_s), (mix_gain_h, mix_gain), (out_w_h, out_w),
             )
         )
@@ -145,6 +145,12 @@
 
     for load in (loads[0], *loads[2:]):
         load.wait()
+    for k in range(4):
+
+        @pl.when(x == k)
+        def _(k=k):
+            maps_w[...] = all_maps[:, k, :]
+
     pl.semaphore_wait(barrier, 32 - 2 * own_leg.astype(jnp.int32))
 
     for i in range(8):
@@ -318,19 +324,19 @@
     product(2)
     hop(1, 0)
     hop(0, 2)
+    hop(1, 1)
+    hop(0, 3)
     came(3)
     product(3)
     hop(2, 0)
-    hop(1, 1)
-    hop(0, 3)
-    hop(2, 1)
     hop(1, 2)
     last(0)
+    hop(2, 1)
+    hop(1, 3)
     hop(2, 2)
-    hop(1, 3)
+    last(1)
     hop(2, 3)
     hop(3, 0)
-    last(1)
     last(2)
 
     scale = lax.rsqrt(RV[:, :, :, 256:384].reshape(256, 128)[:, SQ : SQ + 1] * (1.0 / 8192) + EPSILON)
@@ -435,13 +441,15 @@
         send(SO.at[k], SI.at[z], sem_in.at[z], dev(z_=k))
     SI[z] = SO[z]
     hop(3, 3)
+    last(3)
+    gate = RG[...].reshape(256, 256) * scale
+    gate = gate * jax.nn.sigmoid(gate)
+    partly = partly * gate
+    carried = carried * gate
     for o in range(1, 8):
         k = m8(z + o)
         arrived(SI.at[k], sem_in.at[k])
-    outputs = partly + dot(c_cols, SI[...].reshape(128, 256)) * carried
-    last(3)
-    gate = RG[...].reshape(256, 256) * scale
-    gated = outputs * (gate * jax.nn.sigmoid(gate))
+    gated = partly + dot(c_cols, SI[...].reshape(128, 256)) * carried
     GZ[c, z] = (gated * mix_gain[0:1, own_cols]).astype(BF16).reshape(2, 128, 256)
 
     order = [z]
@@ -460,13 +468,6 @@
     )
     for dc, dy in peers:
         send(SQB.at[own_sq], SQB.at[own_sq], sem_sq.at[own_sq], dev(c_=lax.rem(c + dc, 2), y_=m4(y + dy)))
-    for dc, dy in peers:
-        k = 2 * m4(y + dy) + lax.rem(c + dc, 2)
-        arrived(SQB.at[k], sem_sq.at[k])
-    NZ[z] = lax.rsqrt(jnp.sum(SQB[...], axis=0) * (1.0 / 2048) + EPSILON)
-    for o in range(1, 8):
-        send(NZ.at[z], NZ.at[z], sem_nz.at[z], dev(z_=m8(z + o)))
-
     def pass_on(o, i):
         zt = order[o]
         got = GZ.at[c, zt, i]
@@ -477,13 +478,14 @@
             send(got, got, sem_g.at[zt, i], dev(z_=m8(z - sg)))
         send(got, got, sem_gs.at[zt, i], sibling)
 
+    def forward(o):
+        for i in range(2):
+            pass_on(o, i)
+            if o < 7:
+                pass_on(o + 1, i)
+
     def take(o):
         zt = order[o]
-        if o % 2 == 1:
-            for i in range(2):
-                pass_on(o, i)
-                if o < 7:
-                    pass_on(o + 1, i)
         for i in range(2):
             arrived(GZ.at[1 - c, zt, i], sem_gs.at[zt, i])
         if o:
@@ -551,19 +553,47 @@
         else:
             send_or_keep(own, FO.at[o], FR.at[row_block], sem_f.at[row_block], to)
 
-    for tick in range(8 + 2):
-        if tick < 8:
-            take(tick)
-            first_out(tick)
-        if 0 <= tick - 1 < 8 and tick - 1 not in straight:
-            first_relay(tick - 1)
-        if 2 <= tick < 9:
-            second_out(tick - 2)
-        if tick == 8:
-            second_out(7)
-        if 0 <= tick - 3 < 8:
-            finish(tick - 3)
-    finish(7)
+    forward(1)
+    for dc, dy in peers:
+        k = 2 * m4(y + dy) + lax.rem(c + dc, 2)
+        arrived(SQB.at[k], sem_sq.at[k])
+    NZ[z] = lax.rsqrt(jnp.sum(SQB[...], axis=0) * (1.0 / 2048) + EPSILON)
+    for o in range(1, 8):
+        send(NZ.at[z], NZ.at[z], sem_nz.at[z], dev(z_=m8(z + o)))
+    take(0)
+    first_out(0)
+    forward(3)
+    for o in (1, 2):
+        take(o)
+        first_out(o)
+    first_relay(0)
+    forward(5)
+    for o in (3, 4):
+        take(o)
+        first_out(o)
+    first_relay(1)
+    first_relay(2)
+    second_out(0)
+    forward(7)
+    for o in (5, 6):
+        take(o)
+        first_out(o)
+    first_relay(3)
+    first_relay(4)
+    take(7)
+    first_out(7)
+    second_out(1)
+    second_out(2)
+    first_relay(5)
+    second_out(3)
+    second_out(4)
+    for o in range(3):
+        finish(o)
+    second_out(6)
+    second_out(5)
+    second_out(7)
+    for o in (3, 4, 6, 5, 7):
+        finish(o)
 
     for i in range(8):
         arrived(FR.at[i], sem_f.at[i])
@@ -576,7 +606,6 @@
     tokens, norm_gain, gate_proj, value_proj, step_proj, state_proj, conv_value, conv_state, step_bias, decay_rate,
     skip_gain, mix_gain, out_proj, doc_lengths,
 ):
-    maps = lax.dynamic_index_in_dim(state_proj, lax.axis_index("fsdp") // 4, 1, keepdims=False)
     vmem = pl.BlockSpec(memory_space=pltpu.VMEM)
     smem = pl.BlockSpec(memory_space=pltpu.SMEM)
 
@@ -596,12 +625,13 @@
             buf(1, 8192, dtype=F32),
             buf(512, 512),
             buf(512, 512),
-            buf(512, 256),
+            buf(512, 4, 256),
             buf(8, 512),
             buf(4, 512, dtype=F32),
             buf(4, 4, 256, dtype=F32),
             buf(1, 512, dtype=F32),
             buf(512, 512),
+            buf(512, 256),
             buf(8, 16, 512),
             buf(2, 2, 4, 4, 4, 16, 512),
             buf(2, 512, 384),
@@ -639,7 +669,7 @@
         compiler_params=pltpu.CompilerParams(collective_id=0, has_side_effects=True, vmem_limit_bytes=56 * 2**20),
         name="mixer",
     )(
-        tokens, norm_gain.reshape(1, -1), gate_proj, value_proj, maps, step_proj.T, conv_value, conv_state, mix_gain.reshape(1, -1),
+        tokens, norm_gain.reshape(1, -1), gate_proj, value_proj, state_proj, step_proj.T, conv_value, conv_state, mix_gain.reshape(1, -1),
         out_proj, step_bias, decay_rate, skip_gain, doc_lengths,
     )
 

time: 131 us -> 127 us (0.969)
  local copies, waits for them, and re-layouts: 4.07 us -> 1.57 us
    unnamed x4 -> x1, local copies, waits for them, and re-layouts: 3.53 us -> 1.57 us
where the time goes in v4:
time: 127 us
  Pallas kernels  125 us (98%)
  local copies, waits for them, and re-layouts  1.57 us (1%)
    pallas_call x1, Pallas kernels, local(): pl.pallas_call(body, out_shape=jax.ShapeDtypeStruct((128, 512), BF16), in...  125 us

profile of v4, /device:TPU:4, one launch (start us, length us, event | category | flops | bytes accessed | tf_op | source)
XLA Modules:
  0.0 127.1 jit_solution(12807187972127322984)
XLA Ops:
  0.0 125.5 %mixer.1 = bf16[128,512]{1,0:T(8,128)(2,1)} custom-call(bf16[128,512]{1,0:T(8,128)(2,1)} %tok_h.1, f32[1,8192]{1,0:T(1,128)} %bitcast.3, bf16[512,512]{1,0:T(8,128)(2,1)} %gate_h.1, bf16[512,512]{1,0:T(8,128)(2,1)} %value_h.1, bf16[512,4,256]{2,1,0:T(4,128)(2,1)} %maps_h.1, bf16[8,512]{1,0:T(8,128)(2,1)} %bitcast.4, f32[4,512]{1,0:T(4,128)} %conv_v_h.1, ...), custom_call_target="tpu_custom_call" | custom-call | tf_op jit(solution)/shard_map/mixer/pallas_call | solution.py:618
  125.5 1.6 %copy.16 = bf16[128,512]{1,0:T(8,128)(2,1)} copy(bf16[128,512]{1,0:T(8,128)(2,1)} %mixer.1) | data formatting | bytes 262144

commit v5 on v4

--- a/solution.py
+++ b/solution.py
@@ -14,7 +14,8 @@
 WIDE = 640
 STEP0 = 32
 SQ = 40
-SENDS = 320
+SENDS = 400
+PIECES = 4
 
 
 def dot(a, b, precision=None):
@@ -26,7 +27,7 @@
     bias, rate, skip, docs,
     out,
     tok, gain, gate_w, value_w, all_maps, step_w, conv_v, conv_s, mix_gain, out_w, maps_w,
-    XI, X, WV, WG, SV, SG, PV, PG, S0L, S0S, R0L, R0S, S1L, S1S, R1L, R1S, S2L, S2S, R2L, R2S, S3L, S3S, R3L, R3S, RV, RG,
+    XI, X, WV, WG, SV, SG, PV, PG, S0L, S0S, R0L, R0S, S1L, S1S, R1L, R1S, S2L, S2S, R2L, R2S, S3L, S3S, R3L, R3S, S4L, S4S, R4L, R4S, RV, RG,
     HS, HR, EXT, BC, ST, SR, SO, SI, SQB, NZ, GZ, T, Q, A1, B1, C1, RA1, RB1, RC1,
     A2, B2, C2, RA2, RB2, RC2, FO, FR,
     sem_load, sem_send, sem_i, sem_a, sem_y, sem_x, sem_s, sem_w, sem_l, sem_sh, sem_h, sem_bc, sem_st, sem_in, sem_sq,
@@ -223,11 +224,13 @@
         mine = X.at[c, h, a, b]
         send(mine, mine, sem_y.at[h, b], to(m4(b + 1)))
         send(mine, mine, sem_y.at[h, b], to(m4(b - 1)))
+    for h, (_, _, b, _) in enumerate(legs):
         spread(h, b)
     for h, (a, _, b, to) in enumerate(legs):
         near = X.at[c, h, a, m4(b - sg)]
         trailing(h, m4(b - sg))
         send(near, near, sem_y.at[h, m4(b - sg)], to(m4(b + sg)))
+    for h, (_, _, b, _) in enumerate(legs):
         spread(h, m4(b - sg))
         trailing(h, m4(b + sg))
         spread(h, m4(b + sg))
@@ -265,9 +268,10 @@
 
     rings = [
         (0, 1, "all", S0L, S0S, R0L, R0S),
-        (1, 2, "values", S1L, S1S, R1L, R1S),
-        (3, 1, "values", S2L, S2S, R2L, R2S),
-        (1, 3, "gate", S3L, S3S, R3L, R3S),
+        (1, 1, "values", S1L, S1S, R1L, R1S),
+        (2, 1, "values", S2L, S2S, R2L, R2S),
+        (3, 1, "values", S3L, S3S, R3L, R3S),
+        (1, 3, "gate", S4L, S4S, R4L, R4S),
     ]
 
     def pieces(r, d):
@@ -321,23 +325,28 @@
     came(1)
     came(2)
     product(1)
+    hop(1, 0)
     product(2)
-    hop(1, 0)
+    hop(2, 0)
     hop(0, 2)
     hop(1, 1)
+    hop(2, 1)
     hop(0, 3)
     came(3)
     product(3)
-    hop(2, 0)
+    hop(3, 0)
     hop(1, 2)
+    hop(2, 2)
+    hop(3, 1)
+    hop(1, 3)
+    hop(2, 3)
+    hop(3, 2)
     last(0)
-    hop(2, 1)
-    hop(1, 3)
-    hop(2, 2)
     last(1)
-    hop(2, 3)
-    hop(3, 0)
+    hop(3, 3)
     last(2)
+    hop(4, 0)
+    last(3)
 
     scale = lax.rsqrt(RV[:, :, :, 256:384].reshape(256, 128)[:, SQ : SQ + 1] * (1.0 / 8192) + EPSILON)
     raw = (RV[...].reshape(256, 384) * scale).astype(BF16)
@@ -373,7 +382,7 @@
 
     arrived(HR, sem_h)
     EXT[0:16] = HR[...].astype(F32)
-    hop(3, 1)
+    hop(4, 1)
 
     def conv(lo, width, taps):
         acc = jnp.zeros((256, width), F32)
@@ -408,7 +417,7 @@
     for dc, dy in peers:
         pc, py = lax.rem(c + dc, 2), m4(y + dy)
         arrived(BC.at[pc, py], sem_bc.at[4 * pc + py])
-    hop(3, 2)
+    hop(4, 2)
     b_rows = BC[0].reshape(128, 256)
     c_cols = jnp.transpose(BC[1].reshape(128, 256).astype(F32)).astype(BF16)
 
@@ -428,6 +437,7 @@
         parts.append(dot(mixing, stepped[:, 128 * (i // 2) : 128 * (i // 2) + 128]))
     intra = jnp.concatenate([jnp.where(low, parts[0], parts[1]), jnp.where(low, parts[2], parts[3])], axis=1)
     partly = intra + skip_row * inputs
+    hop(4, 3)
 
     for o in range(1, 8):
         k = m8(z + o)
@@ -440,8 +450,7 @@
         k = m8(z + o)
         send(SO.at[k], SI.at[z], sem_in.at[z], dev(z_=k))
     SI[z] = SO[z]
-    hop(3, 3)
-    last(3)
+    last(4)
     gate = RG[...].reshape(256, 256) * scale
     gate = gate * jax.nn.sigmoid(gate)
     partly = partly * gate
@@ -450,13 +459,13 @@
         k = m8(z + o)
         arrived(SI.at[k], sem_in.at[k])
     gated = partly + dot(c_cols, SI[...].reshape(128, 256)) * carried
-    GZ[c, z] = (gated * mix_gain[0:1, own_cols]).astype(BF16).reshape(2, 128, 256)
+    GZ[c, z] = (gated * mix_gain[0:1, own_cols]).astype(BF16).reshape(PIECES, 256 // PIECES, 256)
 
     order = [z]
     for k in range(1, 4):
         order += [m8(z - k * sg), m8(z + k * sg)]
     order.append(m8(z + 4))
-    for i in range(2):
+    for i in range(PIECES):
         block = GZ.at[c, z, i]
         send(block, block, sem_g.at[z, i], dev(z_=m8(z + sg)))
         send(block, block, sem_g.at[z, i], dev(z_=m8(z - sg)))
@@ -479,14 +488,14 @@
         send(got, got, sem_gs.at[zt, i], sibling)
 
     def forward(o):
-        for i in range(2):
+        for i in range(PIECES):
             pass_on(o, i)
             if o < 7:
                 pass_on(o + 1, i)
 
     def take(o):
         zt = order[o]
-        for i in range(2):
+        for i in range(PIECES):
             arrived(GZ.at[1 - c, zt, i], sem_gs.at[zt, i])
         if o:
             arrived(NZ.at[zt], sem_nz.at[zt])
@@ -641,7 +650,7 @@
             buf(4, 2, 4, 4, 16, 384, dtype=F32),
             buf(4, 2, 4, 4, 16, 256, dtype=F32),
         ]
-        + [buf(k, n, 4, 16, w) for n, w in ((1, 640), (2, 384), (1, 384), (3, 256)) for k in (4, 3, 4, 3)]
+        + [buf(k, n, 4, 16, w) for n, w in ((1, 640), (1, 384), (1, 384), (1, 384), (3, 256)) for k in (4, 3, 4, 3)]
         + [
             buf(4, 4, 16, 384, dtype=F32),
             buf(4, 4, 16, 256, dtype=F32),
@@ -655,7 +664,7 @@
             buf(8, 16, 256),
             buf(8, 8, 256, dtype=F32),
             buf(8, 8, 256, dtype=F32),
-            buf(2, 8, 2, 128, 256),
+            buf(2, 8, PIECES, 256 // PIECES, 256),
             buf(8, 4, 4, 16, 512, dtype=F32),
             buf(8, 4, 16, 512, dtype=F32),
         ]
@@ -663,8 +672,8 @@
         + [buf(8, 16, 512)] * 6
         + [buf(8, 16, 512)] * 2
         + [
-            dma(10), dma(SENDS), dma(8), dma(8), dma(2, 4), dma(2, 4, 4), dma(2, 4), dma(2), dma(4, 4), dma(4, 3), dma(), dma(8),
-            dma(8), dma(8), dma(8), dma(8), dma(8, 2), dma(8, 2), dma(8, 3), dma(8, 3), dma(8),
+            dma(10), dma(SENDS), dma(8), dma(8), dma(2, 4), dma(2, 4, 4), dma(2, 4), dma(2), dma(5, 4), dma(5, 3), dma(), dma(8),
+            dma(8), dma(8), dma(8), dma(8), dma(8, PIECES), dma(8, PIECES), dma(8, 3), dma(8, 3), dma(8),
         ],
         compiler_params=pltpu.CompilerParams(collective_id=0, has_side_effects=True, vmem_limit_bytes=56 * 2**20),
         name="mixer",

time: 127 us -> 126 us (level)
  no operation moved by 1% of the time
where the time goes in v5:
time: 126 us
  Pallas kernels  125 us (99%)
  local copies, waits for them, and re-layouts  1.57 us (1%)
    pallas_call x1, Pallas kernels, local(): pl.pallas_call(body, out_shape=jax.ShapeDtypeStruct((128, 512), BF16), in...  125 us

profile of v5, /device:TPU:4, one launch (start us, length us, event | category | flops | bytes accessed | tf_op | source)
XLA Modules:
  0.0 126.4 jit_solution(921582625747148400)
XLA Ops:
  0.0 124.8 %mixer.1 = bf16[128,512]{1,0:T(8,128)(2,1)} custom-call(bf16[128,512]{1,0:T(8,128)(2,1)} %tok_h.1, f32[1,8192]{1,0:T(1,128)} %bitcast.3, bf16[512,512]{1,0:T(8,128)(2,1)} %gate_h.1, bf16[512,512]{1,0:T(8,128)(2,1)} %value_h.1, bf16[512,4,256]{2,1,0:T(4,128)(2,1)} %maps_h.1, bf16[8,512]{1,0:T(8,128)(2,1)} %bitcast.4, f32[4,512]{1,0:T(4,128)} %conv_v_h.1, ...), custom_call_target="tpu_custom_call" | custom-call | tf_op jit(solution)/shard_map/mixer/pallas_call | solution.py:627
  124.8 1.6 %copy.16 = bf16[128,512]{1,0:T(8,128)(2,1)} copy(bf16[128,512]{1,0:T(8,128)(2,1)} %mixer.1) | data formatting | bytes 262144

commit v6 on v5

--- a/solution.py
+++ b/solution.py
@@ -28,10 +28,10 @@
     out,
     tok, gain, gate_w, value_w, all_maps, step_w, conv_v, conv_s, mix_gain, out_w, maps_w,
     XI, X, WV, WG, SV, SG, PV, PG, S0L, S0S, R0L, R0S, S1L, S1S, R1L, R1S, S2L, S2S, R2L, R2S, S3L, S3S, R3L, R3S, S4L, S4S, R4L, R4S, RV, RG,
-    HS, HR, EXT, BC, ST, SR, SO, SI, SQB, NZ, GZ, T, Q, A1, B1, C1, RA1, RB1, RC1,
+    HS, HR, EXT, BC, ST, SR, PB, SO, SI, SQB, NZ, GZ, T, Q, A1, B1, C1, RA1, RB1, RC1,
     A2, B2, C2, RA2, RB2, RC2, FO, FR,
     sem_load, sem_send, sem_i, sem_a, sem_y, sem_x, sem_s, sem_w, sem_l, sem_sh, sem_h, sem_bc, sem_st, sem_in, sem_sq,
-    sem_nz, sem_g, sem_gs, sem_1, sem_2, sem_f,
+    sem_p, sem_nz, sem_g, sem_gs, sem_1, sem_2, sem_f,
 ):
     s = lax.axis_index("seq")
     f = lax.axis_index("fsdp")
@@ -101,6 +101,8 @@
     def greet(to):
         pl.semaphore_signal(barrier, inc=1, device_id=to, device_id_type=MESH)
 
+    for o in (4, 3, 5, 2, 6, 1, 7):
+        greet(dev(z_=m8(z + o)))
     for i in range(8):
         for to, at in (((2 * z + lax.rem(f, 2), 8 * c + i), 8 * c + i), ((2 * z + lax.div(x, 2), 2 * i + c), 2 * i + c)):
 
@@ -108,8 +110,6 @@
             def _(to=to):
                 greet(to)
 
-    for o in range(1, 8):
-        greet(dev(z_=m8(z + o)))
     for dc, dy in peers:
         greet(dev(c_=lax.rem(c + dc, 2), y_=m4(y + dy)))
     greet(dev(x_=m4(x + 1)))
@@ -126,6 +126,24 @@
     ]
     for load in loads:
         load.start()
+    loads[0].wait()
+    pl.semaphore_wait(barrier, 32 - 2 * own_leg.astype(jnp.int32))
+
+    for i in range(8):
+        send_or_keep(
+            own_leg & (f == 8 * c + i),
+            tok.at[pl.ds(16 * i, 16)], XI.at[lax.div(f, 2)], sem_i.at[lax.div(f, 2)],
+            (2 * z + lax.rem(f, 2), 8 * c + i),
+        )
+    upper = lax.div(z, 4)
+    lead, trail = x + upper * (y - x), y + upper * (x - y)
+    for o in (4, 3, 5, 2, 6, 1, 7):
+        to = m8(z + o)
+        arrived(XI.at[to], sem_i.at[to])
+        send(XI.at[to], X.at[c, upper, lead, trail, lax.rem(z, 4)], sem_a.at[z], dev(z_=to))
+    arrived(XI.at[z], sem_i.at[z])
+    pltpu.make_async_copy(XI.at[z], X.at[c, upper, lead, trail, lax.rem(z, 4)], sem_a.at[z]).start()
+
     loads[1].wait()
 
     gain_col = jnp.transpose(
@@ -144,7 +162,7 @@
         ref_v[:, 256:384] = (extra * gain_col).astype(BF16)
         ref_g[...] = (gate_w[:, cols].astype(F32) * gain_col).astype(BF16)
 
-    for load in (loads[0], *loads[2:]):
+    for load in loads[2:]:
         load.wait()
     for k in range(4):
 
@@ -152,26 +170,10 @@
         def _(k=k):
             maps_w[...] = all_maps[:, k, :]
 
-    pl.semaphore_wait(barrier, 32 - 2 * own_leg.astype(jnp.int32))
-
-    for i in range(8):
-        send_or_keep(
-            own_leg & (f == 8 * c + i),
-            tok.at[pl.ds(16 * i, 16)], XI.at[lax.div(f, 2)], sem_i.at[lax.div(f, 2)],
-            (2 * z + lax.rem(f, 2), 8 * c + i),
-        )
     rows_of(1 - c, SV, SG)
     send(SV, WV.at[c], sem_w.at[0], sibling)
     send(SG, WG.at[c], sem_w.at[1], sibling)
     rows_of(c, WV.at[c], WG.at[c])
-    upper = lax.div(z, 4)
-    lead, trail = x + upper * (y - x), y + upper * (x - y)
-    for o in (4, 3, 5, 2, 6, 1, 7):
-        to = m8(z + o)
-        arrived(XI.at[to], sem_i.at[to])
-        send(XI.at[to], X.at[c, upper, lead, trail, lax.rem(z, 4)], sem_a.at[z], dev(z_=to))
-    arrived(XI.at[z], sem_i.at[z])
-    pltpu.make_async_copy(XI.at[z], X.at[c, upper, lead, trail, lax.rem(z, 4)], sem_a.at[z]).start()
 
     lane8 = lax.broadcasted_iota(jnp.int32, (8, 128), 1)
     starts = jnp.full((8, 128), 1 << 20, jnp.int32)
@@ -224,13 +226,11 @@
         mine = X.at[c, h, a, b]
         send(mine, mine, sem_y.at[h, b], to(m4(b + 1)))
         send(mine, mine, sem_y.at[h, b], to(m4(b - 1)))
-    for h, (_, _, b, _) in enumerate(legs):
         spread(h, b)
     for h, (a, _, b, to) in enumerate(legs):
         near = X.at[c, h, a, m4(b - sg)]
         trailing(h, m4(b - sg))
         send(near, near, sem_y.at[h, m4(b - sg)], to(m4(b + sg)))
-    for h, (_, _, b, _) in enumerate(legs):
         spread(h, m4(b - sg))
         trailing(h, m4(b + sg))
         spread(h, m4(b + sg))
@@ -349,9 +349,9 @@
     last(3)
 
     scale = lax.rsqrt(RV[:, :, :, 256:384].reshape(256, 128)[:, SQ : SQ + 1] * (1.0 / 8192) + EPSILON)
+    HS[...] = (RV[3, 3] * scale[240:256]).astype(BF16)
+    send(HS, HR, sem_h, dev(z_=m8(z + 1)))
     raw = (RV[...].reshape(256, 384) * scale).astype(BF16)
-    HS[...] = raw[240:256]
-    send(HS, HR, sem_h, dev(z_=m8(z + 1)))
     EXT[16:272] = raw.astype(F32)
 
     raw_step = RV[:, :, :, 256:384].reshape(256, 128) * scale + bias_row
@@ -378,7 +378,9 @@
     step_wide = expand(step)
     tail = expand(jnp.where(t_col >= start_last, jnp.exp(end - cum), 0.0))
     carried = expand(jnp.where(start_of < first, jnp.exp(cum), 0.0))
-    passing = expand(jnp.where(start_last < first, jnp.exp(end), 0.0))
+    PB[z] = jnp.broadcast_to(expand(jnp.where(start_last < first, jnp.exp(end), 0.0)), (8, 256))
+    for o in range(1, 8):
+        send(PB.at[z], PB.at[z], sem_p.at[z], dev(z_=m8(z + o)))
 
     arrived(HR, sem_h)
     EXT[0:16] = HR[...].astype(F32)
@@ -422,8 +424,7 @@
     c_cols = jnp.transpose(BC[1].reshape(128, 256).astype(F32)).astype(BF16)
 
     state = dot(b_rows, to_end).astype(BF16)
-    ST[:, 0:16] = state.reshape(8, 16, 256)
-    ST[:, 16:32] = jnp.broadcast_to(passing.astype(BF16)[None], (8, 16, 256))
+    ST[...] = state.reshape(8, 16, 256)
     for o in range(1, 8):
         k = m8(z + o)
         send(ST.at[k], SR.at[z], sem_st.at[z], dev(z_=k))
@@ -442,10 +443,11 @@
     for o in range(1, 8):
         k = m8(z + o)
         arrived(SR.at[k], sem_st.at[k])
+        arrived(PB.at[k], sem_p.at[k])
     incoming = jnp.zeros((16, 256), F32)
     for i in range(8):
         SO[i] = incoming.astype(BF16)
-        incoming = SR[i, 16:32].astype(F32) * incoming + SR[i, 0:16].astype(F32)
+        incoming = PB[i, 0:1] * incoming + SR[i].astype(F32)
     for o in range(1, 8):
         k = m8(z + o)
         send(SO.at[k], SI.at[z], sem_in.at[z], dev(z_=k))
@@ -658,8 +660,9 @@
             buf(16, 384),
             buf(272, 384, dtype=F32),
             buf(2, 4, 32, 256),
-            buf(8, 32, 256),
-            buf(8, 32, 256),
+            buf(8, 16, 256),
+            buf(8, 16, 256),
+            buf(8, 8, 256, dtype=F32),
             buf(8, 16, 256),
             buf(8, 16, 256),
             buf(8, 8, 256, dtype=F32),
@@ -673,7 +676,7 @@
         + [buf(8, 16, 512)] * 2
         + [
             dma(10), dma(SENDS), dma(8), dma(8), dma(2, 4), dma(2, 4, 4), dma(2, 4), dma(2), dma(5, 4), dma(5, 3), dma(), dma(8),
-            dma(8), dma(8), dma(8), dma(8), dma(8, PIECES), dma(8, PIECES), dma(8, 3), dma(8, 3), dma(8),
+            dma(8), dma(8), dma(8), dma(8), dma(8), dma(8, PIECES), dma(8, PIECES), dma(8, 3), dma(8, 3), dma(8),
         ],
         compiler_params=pltpu.CompilerParams(collective_id=0, has_side_effects=True, vmem_limit_bytes=56 * 2**20),
         name="mixer",

time: 126 us -> 126 us (level)
  no operation moved by 1% of the time
where the time goes in v6:
time: 126 us
  Pallas kernels  125 us (99%)
  local copies, waits for them, and re-layouts  1.57 us (1%)
    pallas_call x1, Pallas kernels, local(): pl.pallas_call(body, out_shape=jax.ShapeDtypeStruct((128, 512), BF16), in...  125 us

profile of v6, /device:TPU:4, one launch (start us, length us, event | category | flops | bytes accessed | tf_op | source)
XLA Modules:
  0.0 126.1 jit_solution(4379245009933819314)
XLA Ops:
  0.0 124.6 %mixer.1 = bf16[128,512]{1,0:T(8,128)(2,1)} custom-call(bf16[128,512]{1,0:T(8,128)(2,1)} %tok_h.1, f32[1,8192]{1,0:T(1,128)} %bitcast.3, bf16[512,512]{1,0:T(8,128)(2,1)} %gate_h.1, bf16[512,512]{1,0:T(8,128)(2,1)} %value_h.1, bf16[512,4,256]{2,1,0:T(4,128)(2,1)} %maps_h.1, bf16[8,512]{1,0:T(8,128)(2,1)} %bitcast.4, f32[4,512]{1,0:T(4,128)} %conv_v_h.1, ...), custom_call_target="tpu_custom_call" | custom-call | tf_op jit(solution)/shard_map/mixer/pallas_call | solution.py:629
  124.6 1.6 %copy.16 = bf16[128,512]{1,0:T(8,128)(2,1)} copy(bf16[128,512]{1,0:T(8,128)(2,1)} %mixer.1) | data formatting | bytes 262144

commit v7 on v6

--- a/solution.py
+++ b/solution.py
@@ -28,10 +28,10 @@
     out,
     tok, gain, gate_w, value_w, all_maps, step_w, conv_v, conv_s, mix_gain, out_w, maps_w,
     XI, X, WV, WG, SV, SG, PV, PG, S0L, S0S, R0L, R0S, S1L, S1S, R1L, R1S, S2L, S2S, R2L, R2S, S3L, S3S, R3L, R3S, S4L, S4S, R4L, R4S, RV, RG,
-    HS, HR, EXT, BC, ST, SR, PB, SO, SI, SQB, NZ, GZ, T, Q, A1, B1, C1, RA1, RB1, RC1,
+    HS, HR, EXT, BC, BP, ST, SR, PB, SO, SI, SQB, NZ, GZ, T, Q, A1, B1, C1, RA1, RB1, RC1,
     A2, B2, C2, RA2, RB2, RC2, FO, FR,
     sem_load, sem_send, sem_i, sem_a, sem_y, sem_x, sem_s, sem_w, sem_l, sem_sh, sem_h, sem_bc, sem_st, sem_in, sem_sq,
-    sem_p, sem_nz, sem_g, sem_gs, sem_1, sem_2, sem_f,
+    sem_p, sem_bp, sem_nz, sem_g, sem_gs, sem_1, sem_2, sem_f,
 ):
     s = lax.axis_index("seq")
     f = lax.axis_index("fsdp")
@@ -187,6 +187,14 @@
     start_of = jnp.max(jnp.where(starts <= t_wide, starts, 0.0), axis=1, keepdims=True)
     t_col = t_wide[:, 0:1]
     into = t_col - start_of
+    into_row = jnp.transpose(jnp.broadcast_to(into, (256, 128)))[0:1]
+    group_row = lax.broadcasted_iota(jnp.int32, (4, 256), 0) == x
+    tap_row = lax.broadcasted_iota(jnp.int32, (128, 256), 0)
+    map_taps = jnp.zeros((128, 256), F32)
+    for k in range(4):
+        own_taps = jnp.sum(jnp.where(group_row, conv_s[k], 0.0), axis=0, keepdims=True)
+        map_taps = jnp.where(tap_row == k, own_taps, map_taps)
+    map_taps = jnp.transpose(map_taps)
     bias_row = jnp.zeros((8, 128), F32)
     rate_row = jnp.zeros((8, 128), F32)
     lane_256 = lax.broadcasted_iota(jnp.int32, (8, 256), 1)
@@ -349,12 +357,19 @@
     last(3)
 
     scale = lax.rsqrt(RV[:, :, :, 256:384].reshape(256, 128)[:, SQ : SQ + 1] * (1.0 / 8192) + EPSILON)
-    HS[...] = (RV[3, 3] * scale[240:256]).astype(BF16)
+    HS[...] = (RV[3, 3, :, 0:256] * scale[240:256]).astype(BF16)
     send(HS, HR, sem_h, dev(z_=m8(z + 1)))
-    raw = (RV[...].reshape(256, 384) * scale).astype(BF16)
-    EXT[16:272] = raw.astype(F32)
-
-    raw_step = RV[:, :, :, 256:384].reshape(256, 128) * scale + bias_row
+    extra = RV[:, :, :, 256:384].reshape(256, 128) * scale
+    BC[c, y] = jnp.transpose(extra)[0:32].astype(BF16)
+    for dc, dy in [(0, 0)] + peers:
+        to_c, to_y = lax.rem(c + dc, 2), m4(y + dy)
+        end_of = BC.at[c, y, :, pl.ds(128, 128)]
+        send(end_of, BP.at[c, y], sem_bp.at[4 * c + y], dev(z_=m8(z + 1), c_=to_c, y_=to_y))
+        if (dc, dy) != (0, 0):
+            send(BC.at[c, y], BC.at[c, y], sem_bc.at[4 * c + y], dev(c_=to_c, y_=to_y))
+    EXT[16:272] = (RV[:, :, :, 0:256].reshape(256, 256) * scale).astype(BF16).astype(F32)
+
+    raw_step = extra + bias_row
     step = jnp.maximum(raw_step, 0.0) + jnp.log1p(jnp.exp(-jnp.abs(raw_step)))
     log_decay = -rate_row * step
     order_r = lax.broadcasted_iota(jnp.int32, (256, 256), 0)
@@ -392,24 +407,6 @@
             acc = acc + jnp.where(into >= 3 - k, EXT[13 + k : 269 + k, lo : lo + width], 0.0) * taps[k]
         return acc * jax.nn.sigmoid(acc)
 
-    maps_cols = pl.ds(pl.multiple_of(128 * c, 128), 128)
-    group_row = lax.broadcasted_iota(jnp.int32, (4, 128), 0) == x
-    taps_s = [
-        pltpu.roll(
-            jnp.broadcast_to(
-                jnp.sum(jnp.where(group_row, conv_s[k, :, maps_cols], 0.0), axis=0, keepdims=True), (8, 128)
-            ),
-            turn,
-            1,
-        )[0:1]
-        for k in range(4)
-    ]
-    maps = jnp.transpose(conv(256, 128, taps_s))[0:32].astype(BF16)
-    BC[c, y] = maps
-    for dc, dy in peers:
-        to_c = lax.rem(c + dc, 2)
-        send(BC.at[c, y], BC.at[c, y], sem_bc.at[4 * c + y], dev(c_=to_c, y_=m4(y + dy)))
-
     own_cols = pl.ds(pl.multiple_of(256 * c, 256), 256)
     inputs = conv(0, 256, [conv_v[k : k + 1, own_cols] for k in range(4)]).astype(BF16).astype(F32)
     stepped = inputs * step_wide
@@ -420,8 +417,16 @@
         pc, py = lax.rem(c + dc, 2), m4(y + dy)
         arrived(BC.at[pc, py], sem_bc.at[4 * pc + py])
     hop(4, 2)
-    b_rows = BC[0].reshape(128, 256)
-    c_cols = jnp.transpose(BC[1].reshape(128, 256).astype(F32)).astype(BF16)
+    for at in range(8):
+        arrived(BP.at[at // 4, at % 4], sem_bp.at[at])
+    before = jnp.concatenate([BP[...].reshape(256, 128), BC[...].reshape(256, 256)], axis=1).astype(F32)
+    acc = jnp.zeros((256, 256), F32)
+    for k in range(4):
+        moved = before if k == 3 else pltpu.roll(before, 3 - k, 1)
+        acc = acc + jnp.where(into_row >= 3 - k, moved[:, 128:384], 0.0) * map_taps[:, k : k + 1]
+    maps = (acc * jax.nn.sigmoid(acc)).astype(BF16)
+    b_rows = maps[0:128]
+    c_cols = jnp.transpose(maps[128:256].astype(F32)).astype(BF16)
 
     state = dot(b_rows, to_end).astype(BF16)
     ST[...] = state.reshape(8, 16, 256)
@@ -656,10 +661,11 @@
         + [
             buf(4, 4, 16, 384, dtype=F32),
             buf(4, 4, 16, 256, dtype=F32),
-            buf(16, 384),
-            buf(16, 384),
-            buf(272, 384, dtype=F32),
+            buf(16, 256),
+            buf(16, 256),
+            buf(272, 256, dtype=F32),
             buf(2, 4, 32, 256),
+            buf(2, 4, 32, 128),
             buf(8, 16, 256),
             buf(8, 16, 256),
             buf(8, 8, 256, dtype=F32),
@@ -676,7 +682,7 @@
         + [buf(8, 16, 512)] * 2
         + [
             dma(10), dma(SENDS), dma(8), dma(8), dma(2, 4), dma(2, 4, 4), dma(2, 4), dma(2), dma(5, 4), dma(5, 3), dma(), dma(8),
-            dma(8), dma(8), dma(8), dma(8), dma(8), dma(8, PIECES), dma(8, PIECES), dma(8, 3), dma(8, 3), dma(8),
+            dma(8), dma(8), dma(8), dma(8), dma(8), dma(8), dma(8, PIECES), dma(8, PIECES), dma(8, 3), dma(8, 3), dma(8),
         ],
         compiler_params=pltpu.CompilerParams(collective_id=0, has_side_effects=True, vmem_limit_bytes=56 * 2**20),
         name="mixer",

time: 126 us -> 127 us (level)
  no operation moved by 1% of the time
where the time goes in v7:
time: 127 us
  Pallas kernels  125 us (98%)
  local copies, waits for them, and re-layouts  1.57 us (1%)
    pallas_call x1, Pallas kernels, local(): pl.pallas_call(body, out_shape=jax.ShapeDtypeStruct((128, 512), BF16), in...  125 us

profile of v7, /device:TPU:4, one launch (start us, length us, event | category | flops | bytes accessed | tf_op | source)
XLA Modules:
  0.0 126.9 jit_solution(5186163183855759397)
XLA Ops:
  0.0 125.3 %mixer.1 = bf16[128,512]{1,0:T(8,128)(2,1)} custom-call(bf16[128,512]{1,0:T(8,128)(2,1)} %tok_h.1, f32[1,8192]{1,0:T(1,128)} %bitcast.3, bf16[512,512]{1,0:T(8,128)(2,1)} %gate_h.1, bf16[512,512]{1,0:T(8,128)(2,1)} %value_h.1, bf16[512,4,256]{2,1,0:T(4,128)(2,1)} %maps_h.1, bf16[8,512]{1,0:T(8,128)(2,1)} %bitcast.4, f32[4,512]{1,0:T(4,128)} %conv_v_h.1, ...), custom_call_target="tpu_custom_call" | custom-call | tf_op jit(solution)/shard_map/mixer/pallas_call | solution.py:634
  125.3 1.6 %copy.16 = bf16[128,512]{1,0:T(8,128)(2,1)} copy(bf16[128,512]{1,0:T(8,128)(2,1)} %mixer.1) | data formatting | bytes 262144

commit v8 on v7

--- a/solution.py
+++ b/solution.py
@@ -276,10 +276,10 @@
 
     rings = [
         (0, 1, "all", S0L, S0S, R0L, R0S),
-        (1, 1, "values", S1L, S1S, R1L, R1S),
-        (2, 1, "values", S2L, S2S, R2L, R2S),
+        (1, 1, "all", S1L, S1S, R1L, R1S),
+        (2, 1, "all", S2L, S2S, R2L, R2S),
         (3, 1, "values", S3L, S3S, R3L, R3S),
-        (1, 3, "gate", S4L, S4S, R4L, R4S),
+        (3, 1, "gate", S4L, S4S, R4L, R4S),
     ]
 
     def pieces(r, d):
@@ -346,14 +346,16 @@
     hop(1, 2)
     hop(2, 2)
     hop(3, 1)
+    hop(4, 0)
     hop(1, 3)
     hop(2, 3)
     hop(3, 2)
+    hop(4, 1)
     last(0)
     last(1)
     hop(3, 3)
+    hop(4, 2)
     last(2)
-    hop(4, 0)
     last(3)
 
     scale = lax.rsqrt(RV[:, :, :, 256:384].reshape(256, 128)[:, SQ : SQ + 1] * (1.0 / 8192) + EPSILON)
@@ -399,7 +401,7 @@
 
     arrived(HR, sem_h)
     EXT[0:16] = HR[...].astype(F32)
-    hop(4, 1)
+    hop(4, 3)
 
     def conv(lo, width, taps):
         acc = jnp.zeros((256, width), F32)
@@ -416,7 +418,6 @@
     for dc, dy in peers:
         pc, py = lax.rem(c + dc, 2), m4(y + dy)
         arrived(BC.at[pc, py], sem_bc.at[4 * pc + py])
-    hop(4, 2)
     for at in range(8):
         arrived(BP.at[at // 4, at % 4], sem_bp.at[at])
     before = jnp.concatenate([BP[...].reshape(256, 128), BC[...].reshape(256, 256)], axis=1).astype(F32)
@@ -443,7 +444,6 @@
         parts.append(dot(mixing, stepped[:, 128 * (i // 2) : 128 * (i // 2) + 128]))
     intra = jnp.concatenate([jnp.where(low, parts[0], parts[1]), jnp.where(low, parts[2], parts[3])], axis=1)
     partly = intra + skip_row * inputs
-    hop(4, 3)
 
     for o in range(1, 8):
         k = m8(z + o)
@@ -657,7 +657,7 @@
             buf(4, 2, 4, 4, 16, 384, dtype=F32),
             buf(4, 2, 4, 4, 16, 256, dtype=F32),
         ]
-        + [buf(k, n, 4, 16, w) for n, w in ((1, 640), (1, 384), (1, 384), (1, 384), (3, 256)) for k in (4, 3, 4, 3)]
+        + [buf(k, n, 4, 16, w) for n, w in ((1, 640), (1, 640), (1, 640), (1, 384), (1, 256)) for k in (4, 3, 4, 3)]
         + [
             buf(4, 4, 16, 384, dtype=F32),
             buf(4, 4, 16, 256, dtype=F32),

time: 127 us -> 125 us (0.984)
  Pallas kernels: 125 us -> 123 us
    pallas_call x1, Pallas kernels: 125 us -> 123 us  [local(): pl.pallas_call(body, out_shape=jax.ShapeDtypeStruct((128, 512), BF16), in...]
where the time goes in v8:
time: 125 us; the launch traced here: 124 us
  Pallas kernels  123 us (98%)
  local copies, waits for them, and re-layouts  1.57 us (1%)
    pallas_call x1, Pallas kernels, local(): pl.pallas_call(body, out_shape=jax.ShapeDtypeStruct((128, 512), BF16), in...  123 us

profile of v8, /device:TPU:4, one launch (start us, length us, event | category | flops | bytes accessed | tf_op | source)
XLA Modules:
  0.0 124.4 jit_solution(4218313705944099968)
XLA Ops:
  0.0 122.8 %mixer.1 = bf16[128,512]{1,0:T(8,128)(2,1)} custom-call(bf16[128,512]{1,0:T(8,128)(2,1)} %tok_h.1, f32[1,8192]{1,0:T(1,128)} %bitcast.3, bf16[512,512]{1,0:T(8,128)(2,1)} %gate_h.1, bf16[512,512]{1,0:T(8,128)(2,1)} %value_h.1, bf16[512,4,256]{2,1,0:T(4,128)(2,1)} %maps_h.1, bf16[8,512]{1,0:T(8,128)(2,1)} %bitcast.4, f32[4,512]{1,0:T(4,128)} %conv_v_h.1, ...), custom_call_target="tpu_custom_call" | custom-call | tf_op jit(solution)/shard_map/mixer/pallas_call | solution.py:634
  122.8 1.6 %copy.16 = bf16[128,512]{1,0:T(8,128)(2,1)} copy(bf16[128,512]{1,0:T(8,128)(2,1)} %mixer.1) | data formatting | bytes 262144
